TPU v7x, 32 devices: a whole 2x2x4 slice. The times are simulated.
32 devices in a mesh: dp: 8 (over y, x, core), blk: 4 (over z).
Axes of the slice: x: 2, y: 2, z: 4, core: 2. Of those that a mesh axis runs over, the one named last changes fastest.
Arguments:
- tokens: bfloat16 [16, 16, 48, 768], P('dp', 'blk'), may hold values from -6 to 6
- frame_counts: int32 [16], P('dp'), may hold values from 4 to 16, as said below
- slot_mask: int32 [16, 16, 48], P('dp'), may hold values 0 or 1
- norm1_gain: float32 [768], replicated, may hold values from 0.5 to 1.5
- norm1_bias: float32 [768], replicated, may hold values from -2 to 2
- w_qkv: bfloat16 [768, 2304], replicated, may hold values from -0.21875 to 0.21875
- q_bias: float32 [768], replicated, may hold values from -2 to 2
- v_bias: float32 [768], replicated, may hold values from -2 to 2
- w_out: bfloat16 [768, 768], replicated, may hold values from -1.75 to 1.75
- out_bias: float32 [768], replicated, may hold values from -2 to 2
- norm2_gain: float32 [768], replicated, may hold values from 0.5 to 1.5
- norm2_bias: float32 [768], replicated, may hold values from -2 to 2
- w_up: bfloat16 [768, 3072], replicated, may hold values from -0.21875 to 0.21875
- up_bias: float32 [3072], replicated, may hold values from -2 to 2
- w_down: bfloat16 [3072, 768], replicated, may hold values from -0.109375 to 0.109375
- down_bias: float32 [768], replicated, may hold values from -2 to 2
- norm3_gain: float32 [768], replicated, may hold values from 0.5 to 1.5
- norm3_bias: float32 [768], replicated, may hold values from -2 to 2
- w_align: bfloat16 [768, 1024], replicated, may hold values from -0.21875 to 0.21875
- align_bias: float32 [1024], replicated, may hold values from -2 to 2
- cot_block: bfloat16 [16, 16, 48, 768], P('dp', 'blk'), may hold values from -6 to 6
- cot_align: bfloat16 [16, 16, 48, 1024], P('dp', 'blk'), may hold values from -6 to 6
Outputs:
- block_out: bfloat16 [16, 16, 48, 768], P('dp', 'blk')
- aligned: bfloat16 [16, 16, 48, 1024], P('dp', 'blk')
- grad_tokens: bfloat16 [16, 16, 48, 768], P('dp', 'blk')
- grad_norm1_gain: float32 [768], replicated
- grad_norm1_bias: float32 [768], replicated
- grad_w_qkv: float32 [768, 2304], P('dp')
- grad_q_bias: float32 [768], replicated
- grad_v_bias: float32 [768], replicated
- grad_w_out: float32 [768, 768], P('dp')
- grad_out_bias: float32 [768], replicated
- grad_norm2_gain: float32 [768], replicated
- grad_norm2_bias: float32 [768], replicated
- grad_w_up: float32 [768, 3072], P('dp')
- grad_up_bias: float32 [3072], replicated
- grad_w_down: float32 [3072, 768], P('dp')
- grad_down_bias: float32 [768], replicated
- grad_norm3_gain: float32 [768], replicated
- grad_norm3_bias: float32 [768], replicated
- grad_w_align: float32 [768, 1024], P('dp')
- grad_align_bias: float32 [1024], replicated
Inputs may be any that keep to these rules, and one draw needn't show every extreme that they name: `frame_counts`: each clip has 4, 8 or 16 real frames; in each aligned block of 2 clips (the clips of one index of dp) at least one has 16.
All inputs are finite; a program needn't handle non-finite values. No bound on the sum of `slot_mask` on one device may be relied on, other than what follows from the above.
Results may differ from a plain program's by a relative error of at most 0.013.
Values may be sent and summed in bfloat16 or wider, within the bound.
A program may use at most 192 MiB of HBM per device.

v0:
```python
import math

import jax
import jax.numpy as jnp
from jax import lax
from jax.sharding import PartitionSpec as P

HEADS = 12


EPSILON = 1e-06
SQRT_HALF = 0.7071067811865476
INV_ROOT_TAU = 0.3989422804014327


def norm_forward(values, gain, shift):
    center = values - jnp.mean(values, axis=-1, keepdims=True)
    inverse = lax.rsqrt(jnp.mean(center * center, axis=-1, keepdims=True) + EPSILON)
    normed = center * inverse
    return (normed * gain + shift, normed, inverse)


def norm_backward(upstream, normed, inverse, gain):
    scaled = upstream * gain
    inner = (
        scaled
        - jnp.mean(scaled, axis=-1, keepdims=True)
        - normed * jnp.mean(scaled * normed, axis=-1, keepdims=True)
    )
    return (inverse * inner, jnp.sum(upstream * normed, axis=0), jnp.sum(upstream, axis=0))


def gelu_slope(values):
    return (
        0.5 * (1.0 + lax.erf(values * SQRT_HALF))
        + values * jnp.exp(-0.5 * values * values) * INV_ROOT_TAU
    )


def weight_grad(left, right):
    return lax.dot_general(
        left, right, (((0,), (0,)), ((), ())), preferred_element_type=jnp.float32
    )


def input_grad(upstream, weight):
    return lax.dot_general(
        upstream, weight, (((1,), (1,)), ((), ())), preferred_element_type=jnp.float32
    )


def masked_scores(query_heads, key_heads, key_valid, scale):
    scores = (
        jnp.einsum("cqhd,ckhd->chqk", query_heads, key_heads, preferred_element_type=jnp.float32)
        * scale
    )
    return jnp.where(key_valid, scores, -1e30)


def column_sum(values):
    return jnp.sum(values, axis=0, dtype=jnp.float32)


def local(
    tokens,
    frame_counts,
    slot_mask,
    norm1_gain,
    norm1_bias,
    w_qkv,
    q_bias,
    v_bias,
    w_out,
    out_bias,
    norm2_gain,
    norm2_bias,
    w_up,
    up_bias,
    w_down,
    down_bias,
    norm3_gain,
    norm3_bias,
    w_align,
    align_bias,
    cot_block,
    cot_align,
):
    clip_count, frame_dev, slot_count, width = tokens.shape
    align_width = w_align.shape[1]
    head_size = width // HEADS
    scale = 1.0 / math.sqrt(head_size)
    row_count = clip_count * frame_dev * slot_count
    cycle_pos = lax.axis_index("blk")
    frame_ids = cycle_pos * frame_dev + jnp.arange(frame_dev, dtype=jnp.int32)
    own_slots = lax.dynamic_slice_in_dim(slot_mask, cycle_pos * frame_dev, frame_dev, 1)
    own_mask = (frame_ids[None, :, None] < frame_counts[:, None, None]) & (own_slots > 0)
    visible = own_mask.astype(jnp.float32).reshape(row_count, 1)
    all_frames = jnp.arange(slot_mask.shape[1], dtype=jnp.int32)
    key_valid = (all_frames[None, :, None] < frame_counts[:, None, None]) & (slot_mask > 0)
    key_valid = key_valid.reshape(clip_count, 1, 1, -1)
    inputs = tokens.reshape(row_count, width).astype(jnp.float32)
    normed_one, unit_one, inverse_one = norm_forward(inputs, norm1_gain, norm1_bias)
    normed1 = normed_one.astype(jnp.bfloat16)
    projected = jnp.dot(normed1, w_qkv, preferred_element_type=jnp.float32)
    queries = (projected[:, :width] + q_bias).astype(jnp.bfloat16)
    keys_local = projected[:, width : 2 * width].astype(jnp.bfloat16)
    values_local = (projected[:, 2 * width :] + v_bias).astype(jnp.bfloat16)
    block_shape = (clip_count, frame_dev, slot_count, width)
    heads_shape = (clip_count, -1, HEADS, head_size)
    keys_all, values_all = (
        lax.all_gather(keys_local.reshape(block_shape), "blk", axis=1, tiled=True),
        lax.all_gather(values_local.reshape(block_shape), "blk", axis=1, tiled=True),
    )
    key_heads = keys_all.reshape(heads_shape)
    value_heads = values_all.reshape(heads_shape)
    query_heads = queries.reshape(heads_shape)
    scores = masked_scores(query_heads, key_heads, key_valid, scale)
    top = jnp.max(scores, axis=-1, keepdims=True)
    expo = jnp.exp(scores - top)
    total = jnp.sum(expo, axis=-1, keepdims=True)
    probs_low = (expo / total).astype(jnp.bfloat16)
    attended = jnp.einsum(
        "chqk,ckhd->cqhd", probs_low, value_heads, preferred_element_type=jnp.float32
    )
    attended = attended.astype(jnp.bfloat16).reshape(row_count, width)
    mid = inputs + jnp.dot(attended, w_out, preferred_element_type=jnp.float32) + out_bias
    normed_two, unit_two, inverse_two = norm_forward(mid, norm2_gain, norm2_bias)
    normed2 = normed_two.astype(jnp.bfloat16)
    hidden = jnp.dot(normed2, w_up, preferred_element_type=jnp.float32) + up_bias
    active = jax.nn.gelu(hidden, approximate=False).astype(jnp.bfloat16)
    after = mid + jnp.dot(active, w_down, preferred_element_type=jnp.float32) + down_bias
    block_out = (visible * after).astype(jnp.bfloat16).reshape(block_shape)
    normed_three, unit_three, inverse_three = norm_forward(after, norm3_gain, norm3_bias)
    normed3 = normed_three.astype(jnp.bfloat16)
    target = jnp.dot(normed3, w_align, preferred_element_type=jnp.float32) + align_bias
    aligned = (
        (visible * target)
        .astype(jnp.bfloat16)
        .reshape(clip_count, frame_dev, slot_count, align_width)
    )
    back_align = (visible * cot_align.reshape(row_count, align_width).astype(jnp.float32)).astype(
        jnp.bfloat16
    )
    grad_align_bias = column_sum(back_align)
    grad_w_align = weight_grad(normed3, back_align)
    back_norm3, grad_norm3_gain, grad_norm3_bias = norm_backward(
        input_grad(back_align, w_align), unit_three, inverse_three, norm3_gain
    )
    back_after = visible * cot_block.reshape(row_count, width).astype(jnp.float32) + back_norm3
    back_down = back_after.astype(jnp.bfloat16)
    grad_down_bias = column_sum(back_down)
    grad_w_down = weight_grad(active, back_down)
    back_up = (input_grad(back_down, w_down) * gelu_slope(hidden)).astype(jnp.bfloat16)
    grad_up_bias = column_sum(back_up)
    grad_w_up = weight_grad(normed2, back_up)
    back_norm2, grad_norm2_gain, grad_norm2_bias = norm_backward(
        input_grad(back_up, w_up), unit_two, inverse_two, norm2_gain
    )
    back_mid = back_after + back_norm2
    back_out = back_mid.astype(jnp.bfloat16)
    grad_out_bias = column_sum(back_out)
    grad_w_out = weight_grad(attended, back_out)
    back_attended = input_grad(back_out, w_out).astype(jnp.bfloat16).reshape(heads_shape)
    scores = masked_scores(query_heads, key_heads, key_valid, scale)
    probs = jnp.exp(scores - top) / total
    probs_low = probs.astype(jnp.bfloat16)
    back_probs = jnp.einsum(
        "cqhd,ckhd->chqk", back_attended, value_heads, preferred_element_type=jnp.float32
    )
    spread = jnp.sum(probs * back_probs, axis=-1, keepdims=True)
    back_scores = (probs * (back_probs - spread)).astype(jnp.bfloat16)
    back_queries = (
        jnp.einsum("chqk,ckhd->cqhd", back_scores, key_heads, preferred_element_type=jnp.float32)
        * scale
    )
    back_queries = back_queries.astype(jnp.bfloat16).reshape(row_count, width)
    value_terms = jnp.einsum(
        "chqk,cqhd->ckhd", probs_low, back_attended, preferred_element_type=jnp.float32
    )
    key_terms = (
        jnp.einsum("chqk,cqhd->ckhd", back_scores, query_heads, preferred_element_type=jnp.float32)
        * scale
    )
    whole_shape = (clip_count, -1, slot_count, width)
    key_share, value_share = (
        lax.psum_scatter(
            key_terms.reshape(whole_shape).astype(jnp.bfloat16),
            "blk",
            scatter_dimension=1,
            tiled=True,
        ).astype(jnp.float32),
        lax.psum_scatter(
            value_terms.reshape(whole_shape).astype(jnp.bfloat16),
            "blk",
            scatter_dimension=1,
            tiled=True,
        ).astype(jnp.float32),
    )
    back_keys = key_share.astype(jnp.bfloat16).reshape(row_count, width)
    back_values = value_share.astype(jnp.bfloat16).reshape(row_count, width)
    grad_q_bias = column_sum(back_queries)
    grad_v_bias = column_sum(back_values)
    combined = jnp.concatenate([back_queries, back_keys, back_values], axis=1)
    grad_w_qkv = weight_grad(normed1, combined)
    back_norm1, grad_norm1_gain, grad_norm1_bias = norm_backward(
        input_grad(combined, w_qkv), unit_one, inverse_one, norm1_gain
    )
    grad_tokens = (back_mid + back_norm1).astype(jnp.bfloat16).reshape(block_shape)
    vector_total = lax.psum(
        (
            grad_norm1_gain,
            grad_norm1_bias,
            grad_q_bias,
            grad_v_bias,
            grad_out_bias,
            grad_norm2_gain,
            grad_norm2_bias,
            grad_up_bias,
            grad_down_bias,
            grad_norm3_gain,
            grad_norm3_bias,
            grad_align_bias,
        ),
        ("dp", "blk"),
    )
    row_part = (
        lax.psum_scatter(grad_w_qkv, "dp", scatter_dimension=0, tiled=True),
        lax.psum_scatter(grad_w_out, "dp", scatter_dimension=0, tiled=True),
        lax.psum_scatter(grad_w_up, "dp", scatter_dimension=0, tiled=True),
        lax.psum_scatter(grad_w_down, "dp", scatter_dimension=0, tiled=True),
        lax.psum_scatter(grad_w_align, "dp", scatter_dimension=0, tiled=True),
    )
    matrix_total = (
        lax.psum(row_part[0].astype(jnp.bfloat16), "blk").astype(jnp.float32),
        lax.psum(row_part[1].astype(jnp.bfloat16), "blk").astype(jnp.float32),
        lax.psum(row_part[2].astype(jnp.bfloat16), "blk").astype(jnp.float32),
        lax.psum(row_part[3].astype(jnp.bfloat16), "blk").astype(jnp.float32),
        lax.psum(row_part[4].astype(jnp.bfloat16), "blk").astype(jnp.float32),
    )
    return (
        block_out,
        aligned,
        grad_tokens,
        vector_total[0],
        vector_total[1],
        matrix_total[0],
        vector_total[2],
        vector_total[3],
        matrix_total[1],
        vector_total[4],
        vector_total[5],
        vector_total[6],
        matrix_total[2],
        vector_total[7],
        matrix_total[3],
        vector_total[8],
        vector_total[9],
        vector_total[10],
        matrix_total[4],
        vector_total[11],
    )


def solution(mesh):
    in_specs = (
        P("dp", "blk", None, None),
        P("dp"),
        P("dp", None, None),
        P(),
        P(),
        P(),
        P(),
        P(),
        P(),
        P(),
        P(),
        P(),
        P(),
        P(),
        P(),
        P(),
        P(),
        P(),
        P(),
        P(),
        P("dp", "blk", None, None),
        P("dp", "blk", None, None),
    )
    out_specs = (
        P("dp", "blk", None, None),
        P("dp", "blk", None, None),
        P("dp", "blk", None, None),
        P(),
        P(),
        P("dp", None),
        P(),
        P(),
        P("dp", None),
        P(),
        P(),
        P(),
        P("dp", None),
        P(),
        P("dp", None),
        P(),
        P(),
        P(),
        P("dp", None),
        P(),
    )
    return jax.shard_map(local, mesh=mesh, in_specs=in_specs, out_specs=out_specs, check_vma=False)
```

profile of v0, /device:TPU:0, one launch (start us, length us, event | category | flops | bytes accessed | tf_op | source)
XLA Modules:
  0.0 869.7 jit_solution(5911127261128532920)
XLA Ops:
  21.0 2.8 reshape.282
  23.8 2.8 copy.65
  26.6 2.2 fusion.28
  28.9 40.7 %all-gather.3.cloned.1.call-done = bf16[2,16,48,768]{3,2,1,0:T(8,128)(2,1)} async-done(((bf16[2,4,48,768]{3,2,1,0:T(8,128)(2,1)}), bf16[2,16,48,768]{3,2,1,0:T(8,128)(2,1)}) %all-gather.3.cloned.1.call-update) | async-done | bytes 2359312 | tf_op jit(solution)/shard_map/all_gather | solution.py:112
  69.6 8.2 reshape.259
  77.8 7.5 copy.67
  85.3 35.8 %all-gather.5.cloned.1.call-done = bf16[2,16,48,768]{3,2,1,0:T(8,128)(2,1)} async-done(((bf16[2,4,48,768]{3,2,1,0:T(8,128)(2,1)}), bf16[2,16,48,768]{3,2,1,0:T(8,128)(2,1)}) %all-gather.5.cloned.1.call-update) | async-done | bytes 2359312 | tf_op jit(solution)/shard_map/all_gather | solution.py:111
  121.1 8.2 reshape.262
  129.2 7.4 copy.66
  136.6 12.4 %fusion.62 = (f32[2,12,192]{2,1,0:T(8,128)}, f32[2,12,192,768]{3,2,1,0:T(8,128)}) fusion(pred[2,768]{1,0:T(4,128)(4,1)S(1)} %broadcast_in_dim.18, bf16[2,192,12,64]{1,3,2,0:T(8,128)(2,1)} %copy.65, bf16[2,768,12,64]{1,3,2,0:T(8,128)(2,1)} %copy.66), kind=kOutput, calls=%fused_computation.130 | convolution fusion | flops 467141376 | bytes 17124864 | tf_op jit(solution)/shard_map/sub | solution.py:119
  149.0 8.2 fusion.37
  158.9 3.2 reshape.263
  162.1 2.5 fusion.63
  165.0 13.6 %fusion.7 = (bf16[384,3072]{1,0:T(8,128)(2,1)S(1)}, f32[384,3072]{1,0:T(8,128)S(1)}) fusion(f32[3072]{0:T(1024)S(1)} %copy-done.43, bf16[768,3072]{1,0:T(8,128)(2,1)} %param.34, f32[384,768]{1,0:T(8,128)S(1)} %get-tuple-element.63, f32[768]{0:T(1024)S(1)} %copy-done.23, f32[768]{0:T(1024)S(1)} %copy-done.22, f32[384]{0:T(512)S(1)} %add_rsqrt_fusion.2, ...), kind=kOutput, calls=%fused_computation.14 | convolution fusion | flops 1891270656 | bytes 12997632 | tf_op jit(solution)/shard_map/dot_general | solution.py:129
  184.9 4.3 convert_reduce_fusion
  189.2 2.9 multiply_reduce_fusion.2
  195.7 2.8 reshape.283
  198.4 2.8 copy.70
  201.3 8.3 convert_bitcast_fusion
  209.6 10.0 %multiply_reduce_fusion = (f32[2,12,192]{2,1,0:T(8,128)}, f32[2,12,192,768]{3,2,1,0:T(8,128)}) fusion(f32[2,12,192,768]{3,2,1,0:T(8,128)} %get-tuple-element.61, f32[2,12,192]{2,1,0:T(8,128)S(1)} %copy-done.28, bf16[2,192,12,64]{1,3,2,0:T(8,128)(2,1)S(1)} %copy-done.18, bf16[2,768,12,64]{1,3,2,0:T(8,128)(2,1)S(1)} %copy-done.15), kind=kOutput, calls=%fused_computation.2 | convolution fusion | flops 463597056 | bytes 31297536 | tf_op jit(solution)/shard_map/cqhd,ckhd->chqk/dot_general | solution.py:167
  219.6 10.0 %reshape.275 = bf16[2,16,48,768]{2,1,3,0:T(8,128)(2,1)} reshape(bf16[2,768,12,64]{1,3,2,0:T(8,128)(2,1)} %convert_bitcast_fusion) | data formatting | bytes 4718592 | tf_op jit(solution)/shard_map/convert_element_type | solution.py:193
  229.6 8.0 copy.81
  237.6 10.1 %multiply_convert_fusion = bf16[2,12,192,768]{3,2,1,0:T(8,128)(2,1)S(1)} fusion(f32[2,12,192,768]{3,2,1,0:T(8,128)} %get-tuple-element.71, f32[2,12,192]{2,1,0:T(8,128)} %get-tuple-element.70, f32[2,12,192,768]{3,2,1,0:T(8,128)} %get-tuple-element.61, f32[2,12,192]{2,1,0:T(8,128)} %get-tuple-element.60), kind=kLoop, calls=%fused_computation.1 | loop fusion | flops 14155776 | bytes 35426304 | tf_op jit(solution)/shard_map/convert_element_type | solution.py:171
  247.6 2.9 copy-done.1
  250.5 2.9 fusion.25
  253.4 10.0 %reshape.274 = bf16[2,16,48,768]{2,1,3,0:T(8,128)(2,1)} reshape(bf16[2,768,12,64]{1,3,2,0:T(8,128)(2,1)} %fusion.25) | data formatting | bytes 4718592 | tf_op jit(solution)/shard_map/convert_element_type | solution.py:187
  263.4 8.3 copy.80
  271.8 3.6 fusion.50
  275.5 4.9 fusion.60
  280.5 8.6 fusion.58
  289.2 8.3 fusion.53
  299.4 6.2 convert_reduce_fusion.2
  307.3 3.2 reshape.267
  310.5 132.6 %all-reduce.10.cloned.1.call-done = (bf16[2,16,48,768]{3,2,1,0:T(8,128)(2,1)}, bf16[2,16,48,768]{3,2,1,0:T(8,128)(2,1)}) async-done(((bf16[2,16,48,768]{3,2,1,0:T(8,128)(2,1)}, bf16[2,16,48,768]{3,2,1,0:T(8,128)(2,1)}), (bf16[2,16,48,768]{3,2,1,0:T(8,128)(2,1)}, bf16[2,16,48,768]{3,2,1,0:T(8,128)(2,1)})) %all-reduce.10.cloned.1.call-update) | async-done | bytes 4718608
  444.9 2.2 copy.78
  447.1 2.6 convert_reduce_fusion.5
  449.7 2.2 copy.79
  451.9 6.7 fusion.44
  458.6 29.1 %reduce-scatter.14.cloned.1.call-done = f32[96,768]{1,0:T(8,128)} async-done(((f32[768,768]{1,0:T(8,128)}), f32[96,768]{1,0:T(8,128)}) %reduce-scatter.14.cloned.1.call-update) | async-done | bytes 294928 | tf_op jit(solution)/shard_map/reduce_scatter | solution.py:228
  489.4 48.2 %reduce-scatter.20.cloned.1.call-done = f32[96,1024]{1,0:T(8,128)} async-done(((f32[768,1024]{1,0:T(8,128)}), f32[96,1024]{1,0:T(8,128)}) %reduce-scatter.20.cloned.1.call-update) | async-done | bytes 393232 | tf_op jit(solution)/shard_map/reduce_scatter | solution.py:231
  539.3 78.2 %reduce-scatter.16.cloned.1.call-done = f32[96,3072]{1,0:T(8,128)} async-done(((f32[768,3072]{1,0:T(8,128)}), f32[96,3072]{1,0:T(8,128)}) %reduce-scatter.16.cloned.1.call-update) | async-done | bytes 1179664 | tf_op jit(solution)/shard_map/reduce_scatter | solution.py:229
  619.7 77.9 %reduce-scatter.18.cloned.1.call-done = f32[384,768]{1,0:T(8,128)} async-done(((f32[3072,768]{1,0:T(8,128)}), f32[384,768]{1,0:T(8,128)}) %reduce-scatter.18.cloned.1.call-update) | async-done | bytes 1179664 | tf_op jit(solution)/shard_map/reduce_scatter | solution.py:230
  699.7 66.9 %reduce-scatter.12.cloned.1.call-done = f32[96,2304]{1,0:T(8,128)} async-done(((f32[768,2304]{1,0:T(8,128)}), f32[96,2304]{1,0:T(8,128)}) %reduce-scatter.12.cloned.1.call-update) | async-done | bytes 884752 | tf_op jit(solution)/shard_map/reduce_scatter | solution.py:227
  771.3 3.7 multiply_convert_fusion.4
  775.0 3.5 multiply_reduce_fusion.3
  778.5 43.7 %all-reduce.2 = (f32[768]{0:T(1024)}, f32[768]{0:T(1024)}, f32[768]{0:T(1024)}, f32[768]{0:T(1024)}, f32[768]{0:T(1024)}, /*index=5*/f32[768]{0:T(1024)}, f32[76...) all-reduce(f32[768]{0:T(1024)} %get-tuple-element.24, ...), channel_id=1, replica_groups=mesh['dp'=8,'blk'=4] {'dp','blk'}, use_global_device_ids=true, to_apply=%region_18.19 | all-reduce | flops 11776 | bytes 94208 | tf_op jit(solution)/shard_map/psum | solution.py:209
  823.6 3.0 add_convert_fusion
  826.6 28.7 %all-reduce.8.cloned.1.call-done = (bf16[96,2304]{1,0:T(8,128)(2,1)}, bf16[96,768]{1,0:T(8,128)(2,1)}, bf16[96,3072]{1,0:T(8,128)(2,1)}, bf16[384,768]{1,0:T(8,128)(2,1)}, bf16[96,1024]{1,0:T(8,128)(2,1)}) async-done(((bf16[96,2304]{1,0:T(8,128)(2,1)}, bf16[96,768]{1,0:T(8,128)(2,1)}, bf16[96,3072]{1,0:T(8,128)(2,1)}, bf16[384,768]{1,0:T(8,128)(2,1)}, bf16[96,1024]{1,0:T(8,128)(2,1)}), ...) | async-done | bytes 1966096 | tf_op jit(solution)/shard_map/psum | solution.py:234
  (172 shorter events, 51.7 us)
Async XLA Ops:
  7.2 4.4 copy-start
  7.2 62.4 %all-gather.3.cloned.1.call-start = ((), (), s32[]{:S(2)}) async-start(), calls=%async_computation.5 | async-start | bytes 2949120 | tf_op jit(solution)/shard_map/all_gather | solution.py:112
  8.7 4.5 copy-start.29
  10.2 3.0 copy-start.31
  11.6 3.5 copy-start.40
  11.6 3.4 copy-start.41
  15.0 4.0 copy-start.46
  16.3 104.8 %all-gather.5.cloned.1.call-start = ((), (), s32[]{:S(2)}) async-start(), calls=%async_computation.6 | async-start | bytes 2949120 | tf_op jit(solution)/shard_map/all_gather | solution.py:111
  18.5 424.5 %all-reduce.10.cloned.1.call-start = ((), (), s32[]{:S(2)}) async-start(), calls=%async_computation.13 | async-start | bytes 9437184
  19.9 8.9 %copy-start.24 = (f32[2,4,48]{2,1,0:T(4,128)}, f32[2,4,48]{2,1,0:T(4,128)S(1)}, u32[]{:S(2)}) copy-start(f32[2,4,48]{2,1,0:T(4,128)S(1)} %fusion.47) | copy-start | bytes 4612
  20.0 8.9 %copy-start.33 = (f32[384]{0:T(512)}, f32[384]{0:T(512)S(1)}, u32[]{:S(2)}) copy-start(f32[384]{0:T(512)S(1)} %mul.236) | copy-start | bytes 4612
  157.2 4.9 copy-start.44
  162.1 2.8 copy-start.22
  162.1 2.8 copy-start.23
  162.1 2.9 copy-start.43
  162.1 16.5 %slice-start = ((s8[4718592]{0:T(1024)(128)(4,1)}), s8[4194304]{0:T(1024)(128)(4,1)S(1)}, s32[]{:S(2)}) async-start(s8[4718592]{0:T(1024)(128)(4,1)} %bitcast.104), calls=%async_computation.14 | async-start | bytes 8388608
  164.6 27.4 %copy-start.4 = (f32[384,768]{1,0:T(8,128)}, f32[384,768]{1,0:T(8,128)S(1)}, u32[]{:S(2)}) copy-start(f32[384,768]{1,0:T(8,128)S(1)} %get-tuple-element.63) | copy-start | bytes 3538948
  165.0 13.7 %slice-start.1 = ((s8[4718592]{0:T(1024)(128)(4,1)}), s8[524288]{0:T(1024)(128)(4,1)S(1)}, s32[]{:S(2)}) async-start(s8[4718592]{0:T(1024)(128)(4,1)} %bitcast.104), calls=%async_computation.15 | async-start | bytes 1048576
  165.0 13.7 %copy-start.45 = (f32[768]{0:T(1024)S(1)}, f32[768]{0:T(1024)}, u32[]{:S(2)}) copy-start(f32[768]{0:T(1024)} %param.37) | copy-start | bytes 9220
  178.7 2.5 copy-start.8
  182.9 6.3 slice-start.2
  184.9 7.2 copy-start.5
  184.9 4.3 slice-start.3
  189.2 2.9 copy-start.16
  201.3 8.3 copy-start.15
  201.3 8.3 copy-start.18
  201.3 8.3 copy-start.28
  237.6 12.9 %copy-start.7 = (bf16[2,192,12,64]{1,3,2,0:T(8,128)(2,1)S(1)}, bf16[2,192,12,64]{1,3,2,0:T(8,128)(2,1)}, u32[]{:S(2)}) copy-start(bf16[2,192,12,64]{1,3,2,0:T(8,128)(2,1)} %copy.65) | copy-start | bytes 1769476
  247.6 2.9 copy-start.1
  271.7 216.0 %reduce-scatter.14.cloned.1.call-start = ((), (), s32[]{:S(2)}) async-start(), calls=%async_computation.8 | async-start | bytes 2654208 | tf_op jit(solution)/shard_map/reduce_scatter | solution.py:228
  275.5 262.2 %reduce-scatter.20.cloned.1.call-start = ((), (), s32[]{:S(2)}) async-start(), calls=%async_computation.11 | async-start | bytes 3538944 | tf_op jit(solution)/shard_map/reduce_scatter | solution.py:231
  280.5 337.0 %reduce-scatter.16.cloned.1.call-start = ((), (), s32[]{:S(2)}) async-start(), calls=%async_computation.9 | async-start | bytes 10616832 | tf_op jit(solution)/shard_map/reduce_scatter | solution.py:229
  289.1 408.4 %reduce-scatter.18.cloned.1.call-start = ((), (), s32[]{:S(2)}) async-start(), calls=%async_computation.10 | async-start | bytes 10616832 | tf_op jit(solution)/shard_map/reduce_scatter | solution.py:230
  297.5 469.1 %reduce-scatter.12.cloned.1.call-start = ((), (), s32[]{:S(2)}) async-start(), calls=%async_computation.7 | async-start | bytes 7962624 | tf_op jit(solution)/shard_map/reduce_scatter | solution.py:227
  458.6 396.8 %all-reduce.8.cloned.1.call-start = ((), (), s32[]{:S(2)}) async-start(), calls=%async_computation.12 | async-start | bytes 3932160 | tf_op jit(solution)/shard_map/psum | solution.py:234
  619.7 149.0 %copy-start.25 = (f32[2,4,48]{2,1,0:T(4,128)S(1)}, f32[2,4,48]{2,1,0:T(4,128)}, u32[]{:S(2)}) copy-start(f32[2,4,48]{2,1,0:T(4,128)} %copy-done.24) | copy-start | bytes 4612
  699.7 71.5 %copy-start.27 = (f32[384]{0:T(512)S(1)}, f32[384]{0:T(512)}, u32[]{:S(2)}) copy-start(f32[384]{0:T(512)} %copy-done.26) | copy-start | bytes 4612
  771.2 3.7 copy-start.6
  771.2 3.7 copy-start.12
  771.2 3.7 copy-start.13
  771.3 3.7 copy-start.14
  771.3 3.7 copy-start.30
  771.3 3.7 copy-start.32
  771.3 3.7 copy-start.38
  775.0 3.5 copy-start.36
  775.0 3.5 copy-start.37
  855.4 5.4 copy-start.20
  855.4 6.5 copy-start.19
  (13 other events, 23.4 us)
Sparse Core Ops, SparseCore 0:
  16.4 53.1 all-gather.2
  71.8 49.2 all-gather.4
  271.9 171.1 all-reduce.9
  446.2 41.5 reduce-scatter.13
  491.4 46.2 reduce-scatter.19
  541.0 76.4 reduce-scatter.15
  621.0 76.4 reduce-scatter.17
  701.1 65.5 reduce-scatter.11
  770.7 84.5 all-reduce.7
where the time goes:
time: 875 us; the launch traced here: 870 us
  waiting for transfers between devices  538 us (61%)
  matrix products  117 us (13%)
  local copies, waits for them, and re-layouts  105 us (12%)
  other arithmetic  49.1 us (6%)
  blocking collectives  43.7 us (5%)
  between operations  15.3 us (2%)
    unnamed x10, waiting for transfers between devices  133 us
    reduce_scatter x1, waiting for transfers between devices, local(): lax.psum_scatter(grad_w_up, 'dp', scatter_dimension=0, tiled=True)  78.2 us
    reduce_scatter x1, waiting for transfers between devices, local(): lax.psum_scatter(grad_w_down, 'dp', scatter_dimension=0, tiled=True)  77.9 us
    reduce_scatter x1, waiting for transfers between devices, local(): lax.psum_scatter(grad_w_qkv, 'dp', scatter_dimension=0, tiled=True)  66.9 us
    reduce_scatter x1, waiting for transfers between devices, local(): lax.psum_scatter(grad_w_align, 'dp', scatter_dimension=0, tiled=True)  48.2 us
    psum x1, blocking collectives, local(): lax.psum((grad_norm1_gain, grad_norm1_bias, grad_q_bias, grad_v_bias, gra...  43.7 us
    all_gather x1, waiting for transfers between devices, local(): lax.all_gather(values_local.reshape(block_shape), 'blk', axis=1, tiled=True)  40.7 us
    all_gather x1, waiting for transfers between devices, local(): lax.all_gather(keys_local.reshape(block_shape), 'blk', axis=1, tiled=True)  35.8 us
  transfers between devices with their start and end apart: 9, of which 9 were waited for; matrix products, arithmetic and copies ran while one was open for 12% of the time, Pallas kernels for 0%

commit v1 on v0

--- a/solution.py
+++ b/solution.py
@@ -3,6 +3,8 @@
 import jax
 import jax.numpy as jnp
 from jax import lax
+from jax.experimental import pallas as pl
+from jax.experimental.pallas import tpu as pltpu
 from jax.sharding import PartitionSpec as P
 
 HEADS = 12
@@ -11,6 +13,248 @@
 EPSILON = 1e-06
 SQRT_HALF = 0.7071067811865476
 INV_ROOT_TAU = 0.3989422804014327
+
+
+MESH = pl.DeviceIdType.MESH
+GRID = (8, 4)
+VECTOR_ROWS = 96
+JOBS = (
+    (4, 0, 96, 0, 1024),
+    (3, 0, 192, 0, 768),
+    (3, 192, 192, 0, 768),
+    (2, 0, 96, 0, 1536),
+    (2, 0, 96, 1536, 1536),
+    (1, 0, 96, 0, 768),
+    (0, 0, 96, 0, 768),
+    (0, 0, 96, 768, 768),
+    (0, 0, 96, 1536, 768),
+)
+
+
+def add_into(target, first, second):
+    rows = target.shape[-2]
+    step = 32
+
+    def body(k, _):
+        at = pl.ds(pl.multiple_of(k * step, step), step)
+        target[..., at, :] = (
+            first[..., at, :].astype(jnp.float32) + second[..., at, :].astype(jnp.float32)
+        ).astype(target.dtype)
+        return 0
+
+    lax.fori_loop(0, rows // step, body, 0)
+
+
+def reduce_kernel(*refs):
+    count = len(JOBS)
+    grads = refs[:5]
+    vec_in = refs[5]
+    outs = refs[6:11]
+    vec_out = refs[11]
+    rest = refs[12:]
+    own, got0, got1, got2, gotz = (rest[i * count : (i + 1) * count] for i in range(5))
+    vec_got, local_sem, send0, recv0, send1, recv1, send2, recv2, sendz, recvz, vsend, vrecv = rest[5 * count :]
+
+    dp = lax.axis_index("dp")
+    z = lax.axis_index("blk")
+    core = lax.rem(dp, 2)
+    x = lax.rem(dp // 2, 2)
+    y = dp // 4
+    to_core = (dp + 1 - 2 * core, z)
+    to_x = (dp + 2 - 4 * x, z)
+    to_y = (dp + 4 - 8 * y, z)
+    to_z1 = (dp, z + 1 - 2 * lax.rem(z, 2))
+    to_z2 = (dp, lax.rem(z + 2, 4))
+    to_z3 = (dp, 3 - z)
+    is_mid = (z == 1) | (z == 2)
+    is_end = (z == 0) | (z == 3)
+
+    barrier = pltpu.get_barrier_semaphore()
+    for device in (to_core, to_x, to_y, to_z1, to_z2, to_z3):
+        pl.semaphore_signal(barrier, inc=1, device_id=device, device_id_type=MESH)
+    pl.semaphore_wait(barrier, 6)
+
+    def remote(src, dst, send, recv, device):
+        return pltpu.make_async_remote_copy(
+            src_ref=src, dst_ref=dst, send_sem=send, recv_sem=recv, device_id=device, device_id_type=MESH
+        )
+
+    def pieces(j):
+        matrix, row, rows, column, columns = JOBS[j]
+        half = columns // 2
+        for h in range(2):
+            for chip in range(4):
+                cy, cx = chip // 2, chip % 2
+                first, second = (cx, cy) if h == 0 else (cy, cx)
+                yield h, chip, first, second, pl.ds(row, rows), pl.ds(column + h * half, half)
+
+    def copies0(j):
+        matrix = JOBS[j][0]
+        for h, chip, first, second, rows, columns in pieces(j):
+            yield (
+                remote(
+                    grads[matrix].at[chip, 1 - core, rows, columns],
+                    got0[j].at[h, first, second],
+                    send0.at[j, h * 4 + chip],
+                    recv0.at[j, h * 4 + chip],
+                    to_core,
+                ),
+                pltpu.make_async_copy(
+                    grads[matrix].at[chip, core, rows, columns],
+                    own[j].at[h, first, second],
+                    local_sem.at[j, h * 4 + chip],
+                ),
+            )
+
+    def copies1(j):
+        yield remote(own[j].at[0, 1 - x], got1[j].at[0], send1.at[j, 0], recv1.at[j, 0], to_x)
+        yield remote(own[j].at[1, 1 - y], got1[j].at[1], send1.at[j, 1], recv1.at[j, 1], to_y)
+
+    def copies2(j):
+        yield remote(own[j].at[0, x, 1 - y], got2[j].at[0], send2.at[j, 0], recv2.at[j, 0], to_y)
+        yield remote(own[j].at[1, y, 1 - x], got2[j].at[1], send2.at[j, 1], recv2.at[j, 1], to_x)
+
+    def shares(j):
+        return (own[j].at[0, x, y], own[j].at[1, y, x])
+
+    def copiesz(j, slot, device):
+        for h, share in enumerate(shares(j)):
+            yield remote(share, gotz[j].at[slot, h], sendz.at[j, slot, h], recvz.at[j, slot, h], device)
+
+    def put_out(j, h, value):
+        matrix, row, rows, column, columns = JOBS[j]
+        half = columns // 2
+        outs[matrix][row : row + rows, column + h * half : column + (h + 1) * half] = value
+
+    def stage(j, number):
+        if number == 0:
+            for far, near in copies0(j):
+                far.start()
+                near.start()
+        if number == 1:
+            for far, near in copies0(j):
+                near.wait()
+                far.wait()
+            add_into(own[j], own[j], got0[j])
+            for copy in copies1(j):
+                copy.start()
+        if number == 2:
+            for copy in copies1(j):
+                copy.wait()
+            add_into(own[j].at[0, x], own[j].at[0, x], got1[j].at[0])
+            add_into(own[j].at[1, y], own[j].at[1, y], got1[j].at[1])
+            for copy in copies2(j):
+                copy.start()
+        if number == 3:
+            for copy in copies2(j):
+                copy.wait()
+            for h, share in enumerate(shares(j)):
+                add_into(share, share, got2[j].at[h])
+
+            @pl.when(is_end)
+            def _():
+                for copy in copiesz(j, 0, to_z1):
+                    copy.start()
+        if number == 4:
+
+            @pl.when(is_mid)
+            def _():
+                for copy in copiesz(j, 0, to_z1):
+                    copy.wait_recv()
+                for h, share in enumerate(shares(j)):
+                    add_into(share, share, gotz[j].at[0, h])
+                for copy in copiesz(j, 1, to_z3):
+                    copy.start()
+
+            @pl.when(is_end)
+            def _():
+                for copy in copiesz(j, 0, to_z1):
+                    copy.wait_send()
+        if number == 5:
+
+            @pl.when(is_mid)
+            def _():
+                for copy in copiesz(j, 1, to_z3):
+                    copy.wait()
+                for h, share in enumerate(shares(j)):
+                    add_into(share, share, gotz[j].at[1, h])
+                for copy in copiesz(j, 0, to_z1):
+                    copy.start()
+                for h, share in enumerate(shares(j)):
+                    put_out(j, h, share[...])
+        if number == 6:
+
+            @pl.when(is_mid)
+            def _():
+                for copy in copiesz(j, 0, to_z1):
+                    copy.wait_send()
+
+            @pl.when(is_end)
+            def _():
+                for copy in copiesz(j, 0, to_z1):
+                    copy.wait_recv()
+                for h in range(2):
+                    put_out(j, h, gotz[j][0, h])
+
+    vec_devices = (to_core, to_x, to_y, to_z1, to_z2)
+
+    def vec_copy(k):
+        return remote(vec_out, vec_got.at[k], vsend.at[k], vrecv.at[k], vec_devices[k])
+
+    vec_out[...] = vec_in[...]
+    for step in range(count + 6):
+        if step < 5:
+            vec_copy(step).start()
+        for j in range(count):
+            if 0 <= step - j <= 6:
+                stage(j, step - j)
+        if step < 5:
+            vec_copy(step).wait()
+            vec_out[...] = vec_out[...] + vec_got[step]
+
+
+def reduce_all(grads, vectors):
+    sizes = [vector.shape[0] for vector in vectors]
+    total = sum(sizes)
+    packed = jnp.concatenate(vectors + [jnp.zeros((VECTOR_ROWS * 128 - total,), jnp.float32)])
+    packed = packed.reshape(VECTOR_ROWS, 128)
+    views = [grad.reshape(4, 2, grad.shape[0] // 8, grad.shape[1]) for grad in grads]
+    halves = [(2, 2, 2, job[2], job[4] // 2) for job in JOBS]
+    count = len(JOBS)
+    dma = pltpu.SemaphoreType.DMA
+    scratch = (
+        [pltpu.VMEM(shape, jnp.bfloat16) for shape in halves]
+        + [pltpu.VMEM(shape, jnp.bfloat16) for shape in halves]
+        + [pltpu.VMEM(shape[1:], jnp.bfloat16) for shape in halves]
+        + [pltpu.VMEM(shape[2:], jnp.bfloat16) for shape in halves]
+        + [pltpu.VMEM(shape[1:], jnp.bfloat16) for shape in halves]
+        + [pltpu.VMEM((5, VECTOR_ROWS, 128), jnp.float32)]
+        + [dma((count, 8))] * 3
+        + [dma((count, 2))] * 4
+        + [dma((count, 2, 2))] * 2
+        + [dma((5,))] * 2
+    )
+    vmem = pl.BlockSpec(memory_space=pltpu.VMEM)
+    results = pl.pallas_call(
+        reduce_kernel,
+        name="reduce_grads",
+        out_shape=[
+            jax.ShapeDtypeStruct((view.shape[2], view.shape[3]), jnp.bfloat16) for view in views
+        ]
+        + [jax.ShapeDtypeStruct((VECTOR_ROWS, 128), jnp.float32)],
+        in_specs=[pl.BlockSpec(memory_space=pl.ANY)] * 5 + [vmem],
+        out_specs=[vmem] * 6,
+        scratch_shapes=scratch,
+        compiler_params=pltpu.CompilerParams(
+            collective_id=0, has_side_effects=True, vmem_limit_bytes=56 * 2**20
+        ),
+    )(*views, packed)
+    flat = results[5].reshape(-1)
+    starts = [sum(sizes[:k]) for k in range(len(sizes))]
+    return (
+        [flat[start : start + size] for start, size in zip(starts, sizes)],
+        [result.astype(jnp.float32) for result in results[:5]],
+    )
 
 
 def norm_forward(values, gain, shift):
@@ -206,37 +450,31 @@
         input_grad(combined, w_qkv), unit_one, inverse_one, norm1_gain
     )
     grad_tokens = (back_mid + back_norm1).astype(jnp.bfloat16).reshape(block_shape)
-    vector_total = lax.psum(
-        (
-            grad_norm1_gain,
-            grad_norm1_bias,
-            grad_q_bias,
-            grad_v_bias,
-            grad_out_bias,
-            grad_norm2_gain,
-            grad_norm2_bias,
-            grad_up_bias,
-            grad_down_bias,
-            grad_norm3_gain,
-            grad_norm3_bias,
-            grad_align_bias,
-        ),
-        ("dp", "blk"),
-    )
-    row_part = (
-        lax.psum_scatter(grad_w_qkv, "dp", scatter_dimension=0, tiled=True),
-        lax.psum_scatter(grad_w_out, "dp", scatter_dimension=0, tiled=True),
-        lax.psum_scatter(grad_w_up, "dp", scatter_dimension=0, tiled=True),
-        lax.psum_scatter(grad_w_down, "dp", scatter_dimension=0, tiled=True),
-        lax.psum_scatter(grad_w_align, "dp", scatter_dimension=0, tiled=True),
-    )
-    matrix_total = (
-        lax.psum(row_part[0].astype(jnp.bfloat16), "blk").astype(jnp.float32),
-        lax.psum(row_part[1].astype(jnp.bfloat16), "blk").astype(jnp.float32),
-        lax.psum(row_part[2].astype(jnp.bfloat16), "blk").astype(jnp.float32),
-        lax.psum(row_part[3].astype(jnp.bfloat16), "blk").astype(jnp.float32),
-        lax.psum(row_part[4].astype(jnp.bfloat16), "blk").astype(jnp.float32),
-    )
+    vectors = [
+        grad_norm1_gain,
+        grad_norm1_bias,
+        grad_q_bias,
+        grad_v_bias,
+        grad_out_bias,
+        grad_norm2_gain,
+        grad_norm2_bias,
+        grad_up_bias,
+        grad_down_bias,
+        grad_norm3_gain,
+        grad_norm3_bias,
+        grad_align_bias,
+    ]
+    matrices = [grad_w_qkv, grad_w_out, grad_w_up, grad_w_down, grad_w_align]
+    if (lax.axis_size("dp"), lax.axis_size("blk")) == GRID:
+        vector_total, matrix_total = reduce_all([grad.astype(jnp.bfloat16) for grad in matrices], vectors)
+    else:
+        vector_total = lax.psum(vectors, ("dp", "blk"))
+        matrix_total = [
+            lax.psum(
+                lax.psum_scatter(grad, "dp", scatter_dimension=0, tiled=True).astype(jnp.bfloat16), "blk"
+            ).astype(jnp.float32)
+            for grad in matrices
+        ]
     return (
         block_out,
         aligned,

time: 875 us -> 586 us (0.67)
  waiting for transfers between devices: 538 us -> 211 us
  Pallas kernels: 0 us -> 102 us
  blocking collectives: 43.7 us -> 0 us
  other arithmetic: 49.1 us -> 34.5 us
  matrix products: 117 us -> 108 us
    reduce_scatter x5 -> x0, waiting for transfers between devices: 300 us -> none  [the longest x1 78.2 us: local(): lax.psum_scatter(grad_w_up, 'dp', scatter_dimension=0, tiled=True)]
    pallas_call x0 -> x1, Pallas kernels: none -> 102 us  [reduce_all(): pl.pallas_call(reduce_kernel, name='reduce_grads', out_shape=[jax.ShapeDt...]
    psum x1 -> x0, blocking collectives: 43.7 us -> none  [local(): lax.psum((grad_norm1_gain, grad_norm1_bias, grad_q_bias, grad_v_bias, gra...]
    psum x1 -> x0, waiting for transfers between devices: 28.7 us -> none  [local(): lax.psum(row_part[0].astype(jnp.bfloat16), 'blk').astype(jnp.float32)]
    dot_general x5, matrix products: 32.1 us -> 19.7 us  [weight_grad(): lax.dot_general(left, right, (((0,), (0,)), ((), ())), preferred_element_...]
    convert_element_type x10 -> x5, other arithmetic: 17.3 us -> 6.99 us  [reduce_all(): result.astype(jnp.float32)]
    unnamed x10 -> x4, waiting for transfers between devices: 133 us -> 137 us
  transfers between devices with their start and end apart: 9 -> 3, of which waited for: 9 -> 3; matrix products, arithmetic and copies ran while one was open for 12% -> 11% of each run, Pallas kernels for 0% -> 0%
where the time goes in v1:
time: 586 us; the launch traced here: 581 us
  waiting for transfers between devices  211 us (36%)
  local copies, waits for them, and re-layouts  110 us (19%)
  matrix products  108 us (18%)
  Pallas kernels  102 us (17%)
  other arithmetic  34.5 us (6%)
  between operations  15.6 us (3%)
    unnamed x4, waiting for transfers between devices  137 us
    pallas_call x1, Pallas kernels, reduce_all(): pl.pallas_call(reduce_kernel, name='reduce_grads', out_shape=[jax.ShapeDt...  102 us
    all_gather x1, waiting for transfers between devices, local(): lax.all_gather(keys_local.reshape(block_shape), 'blk', axis=1, tiled=True)  38.1 us
    all_gather x1, waiting for transfers between devices, local(): lax.all_gather(values_local.reshape(block_shape), 'blk', axis=1, tiled=True)  35.7 us
    dot_general x5, matrix products, weight_grad(): lax.dot_general(left, right, (((0,), (0,)), ((), ())), preferred_element_...  19.7 us
    convert_element_type x2, local copies, waits for them, and re-layouts, local(): key_terms.reshape(whole_shape).astype(jnp.bfloat16)  18.3 us
    convert_element_type x2, local copies, waits for them, and re-layouts, local(): value_terms.reshape(whole_shape).astype(jnp.bfloat16)  18 us
    reshape x2, local copies, waits for them, and re-layouts, local(): key_heads = keys_all.reshape(heads_shape)  15.7 us
  transfers between devices with their start and end apart: 3, of which 3 were waited for; matrix products, arithmetic and copies ran while one was open for 11% of the time, Pallas kernels for 0%

profile of v1, /device:TPU:0, one launch (start us, length us, event | category | flops | bytes accessed | tf_op | source)
XLA Modules:
  0.0 581.0 jit_solution(11518672666446669941)
XLA Ops:
  15.9 2.8 fusion.40
  19.4 2.9 reshape.319
  22.2 2.8 copy.65
  28.9 2.3 fusion.28
  31.1 38.1 %all-gather.5.cloned.1.call-done = bf16[2,16,48,768]{3,2,1,0:T(8,128)(2,1)} async-done(((bf16[2,4,48,768]{3,2,1,0:T(8,128)(2,1)}), bf16[2,16,48,768]{3,2,1,0:T(8,128)(2,1)}) %all-gather.5.cloned.1.call-update) | async-done | bytes 2359312 | tf_op jit(solution)/shard_map/all_gather | solution.py:355
  69.3 8.2 %reshape.293 = bf16[2,768,12,64]{3,2,1,0:T(8,128)(2,1)} reshape(bf16[2,16,48,768]{3,2,1,0:T(8,128)(2,1)} %all-gather.5.cloned.1.call-done) | data formatting | bytes 4718592 | tf_op jit(solution)/shard_map/reshape | solution.py:358
  77.4 7.5 %copy.66 = bf16[2,768,12,64]{1,3,2,0:T(8,128)(2,1)} copy(bf16[2,768,12,64]{3,2,1,0:T(8,128)(2,1)} %reshape.293) | data formatting | bytes 4718592 | tf_op jit(solution)/shard_map/reshape | solution.py:358
  85.0 35.7 %all-gather.3.cloned.1.call-done = bf16[2,16,48,768]{3,2,1,0:T(8,128)(2,1)} async-done(((bf16[2,4,48,768]{3,2,1,0:T(8,128)(2,1)}), bf16[2,16,48,768]{3,2,1,0:T(8,128)(2,1)}) %all-gather.3.cloned.1.call-update) | async-done | bytes 2359312 | tf_op jit(solution)/shard_map/all_gather | solution.py:356
  120.7 8.2 %reshape.290 = bf16[2,768,12,64]{3,2,1,0:T(8,128)(2,1)} reshape(bf16[2,16,48,768]{3,2,1,0:T(8,128)(2,1)} %all-gather.3.cloned.1.call-done) | data formatting | bytes 4718592 | tf_op jit(solution)/shard_map/reshape | solution.py:359
  128.8 7.4 %copy.67 = bf16[2,768,12,64]{1,3,2,0:T(8,128)(2,1)} copy(bf16[2,768,12,64]{3,2,1,0:T(8,128)(2,1)} %reshape.290) | data formatting | bytes 4718592 | tf_op jit(solution)/shard_map/reshape | solution.py:359
  136.2 12.4 %fusion.57 = (f32[2,12,192]{2,1,0:T(8,128)}, f32[2,12,192,768]{3,2,1,0:T(8,128)}) fusion(pred[2,768]{1,0:T(4,128)(4,1)S(1)} %broadcast_in_dim.20, bf16[2,192,12,64]{1,3,2,0:T(8,128)(2,1)} %copy.65, bf16[2,768,12,64]{1,3,2,0:T(8,128)(2,1)} %copy.66), kind=kOutput, calls=%fused_computation.155 | convolution fusion | flops 467141376 | bytes 17124864 | tf_op jit(solution)/shard_map/sub | solution.py:363
  148.6 8.1 %fusion.37 = bf16[2,192,12,64]{1,3,2,0:T(8,128)(2,1)S(1)} fusion(bf16[2,768,12,64]{1,3,2,0:T(8,128)(2,1)} %copy.67, f32[2,12,192,768]{3,2,1,0:T(8,128)} %get-tuple-element.66, f32[2,12,192]{2,1,0:T(8,128)} %get-tuple-element.65), kind=kOutput, calls=%fused_computation.65 | convolution fusion | flops 460357632 | bytes 17123328 | tf_op jit(solution)/shard_map/chqk,ckhd->cqhd/dot_general | solution.py:366
  158.5 3.2 reshape.294
  161.7 2.5 fusion.58
  164.6 13.6 %fusion.7 = (bf16[384,3072]{1,0:T(8,128)(2,1)S(1)}, f32[384,3072]{1,0:T(8,128)S(1)}) fusion(f32[3072]{0:T(1024)S(1)} %copy-done.58, bf16[768,3072]{1,0:T(8,128)(2,1)} %param.34, f32[384,768]{1,0:T(8,128)S(1)} %get-tuple-element.68, f32[768]{0:T(1024)S(1)} %copy-done.63, f32[768]{0:T(1024)S(1)} %copy-done.48, f32[384]{0:T(512)S(1)} %add_rsqrt_fusion.2, ...), kind=kOutput, calls=%fused_computation.17 | convolution fusion | flops 1891270656 | bytes 12997632 | tf_op jit(solution)/shard_map/dot_general | solution.py:373
  178.2 2.1 fusion.59
  182.4 2.0 convert_reduce_fusion.3
  184.4 4.4 convert_reduce_fusion
  188.8 2.9 multiply_reduce_fusion.2
  195.3 2.8 reshape.320
  198.1 2.8 copy.70
  201.0 13.8 %multiply_reduce_fusion = (f32[2,12,192]{2,1,0:T(8,128)S(1)}, f32[2,12,192,768]{3,2,1,0:T(8,128)}) fusion(f32[2,12,192,768]{3,2,1,0:T(8,128)} %get-tuple-element.66, f32[2,12,192]{2,1,0:T(8,128)} %get-tuple-element.65, bf16[2,192,12,64]{1,3,2,0:T(8,128)(2,1)} %copy.70, bf16[2,768,12,64]{1,3,2,0:T(8,128)(2,1)} %copy.67), kind=kOutput, calls=%fused_computation.2 | convolution fusion | flops 463597056 | bytes 31297536 | tf_op jit(solution)/shard_map/cqhd,ckhd->chqk/dot_general | solution.py:411
  214.7 8.3 %convert_bitcast_fusion = bf16[2,768,12,64]{1,3,2,0:T(8,128)(2,1)} fusion(bf16[2,192,12,64]{1,3,2,0:T(8,128)(2,1)S(1)} %copy-done.16, f32[2,12,192,768]{3,2,1,0:T(8,128)} %get-tuple-element.66, f32[2,12,192]{2,1,0:T(8,128)S(1)} %copy-done.28), kind=kOutput, calls=%fused_computation.46 | convolution fusion | flops 461242368 | bytes 17123328 | tf_op jit(solution)/shard_map/chqk,cqhd->ckhd/dot_general | solution.py:421
  223.0 6.6 %multiply_convert_fusion = bf16[2,12,192,768]{3,2,1,0:T(8,128)(2,1)S(1)} fusion(f32[2,12,192,768]{3,2,1,0:T(8,128)} %get-tuple-element.76, f32[2,12,192]{2,1,0:T(8,128)S(1)} %get-tuple-element.75, f32[2,12,192,768]{3,2,1,0:T(8,128)S(1)} %bitcast.128, f32[2,12,192]{2,1,0:T(8,128)S(1)} %copy-done.28), kind=kLoop, calls=%fused_computation.1 | loop fusion | flops 14155776 | bytes 35426304 | tf_op jit(solution)/shard_map/convert_element_type | solution.py:415
  229.7 2.9 copy-done.1
  232.5 2.9 fusion.25
  235.4 10.0 %reshape.311 = bf16[2,16,48,768]{2,1,3,0:T(8,128)(2,1)} reshape(bf16[2,768,12,64]{1,3,2,0:T(8,128)(2,1)} %fusion.25) | data formatting | bytes 4718592 | tf_op jit(solution)/shard_map/convert_element_type | solution.py:431
  245.5 8.3 %copy.80 = bf16[2,16,48,768]{3,2,1,0:T(8,128)(2,1)} copy(bf16[2,16,48,768]{2,1,3,0:T(8,128)(2,1)} %reshape.311) | data formatting | bytes 4718592 | tf_op jit(solution)/shard_map/convert_element_type | solution.py:431
  253.8 10.0 %reshape.312 = bf16[2,16,48,768]{2,1,3,0:T(8,128)(2,1)} reshape(bf16[2,768,12,64]{1,3,2,0:T(8,128)(2,1)} %convert_bitcast_fusion) | data formatting | bytes 4718592 | tf_op jit(solution)/shard_map/convert_element_type | solution.py:437
  263.8 8.0 %copy.81 = bf16[2,16,48,768]{3,2,1,0:T(8,128)(2,1)} copy(bf16[2,16,48,768]{2,1,3,0:T(8,128)(2,1)} %reshape.312) | data formatting | bytes 4718592 | tf_op jit(solution)/shard_map/convert_element_type | solution.py:437
  273.7 2.0 convert_reduce_fusion.1
  275.6 6.8 %convert_reduce_fusion.2 = (f32[12,64]{1,0:T(8,128)S(1)}, bf16[2,192,12,64]{1,3,2,0:T(8,128)(2,1)S(1)}) fusion(bf16[2,768,12,64]{1,3,2,0:T(8,128)(2,1)} %copy.66, bf16[2,12,192,768]{3,2,1,0:T(8,128)(2,1)} %copy-done.1), kind=kOutput, calls=%fused_computation.53 | convolution fusion | flops 454163712 | bytes 10030080 | tf_op jit(solution)/shard_map/chqk,ckhd->cqhd/dot_general | solution.py:417
  284.1 3.0 reshape.298
  287.8 3.4 convolution_convert_fusion.4
  291.2 3.2 convolution_convert_fusion.3
  294.5 1.8 multiply_convert_fusion.4
  296.8 4.4 convolution_convert_fusion
  301.2 4.9 convolution_convert_fusion.1
  306.1 137.0 %all-reduce.5.cloned.1.call-done = (bf16[2,16,48,768]{3,2,1,0:T(8,128)(2,1)}, bf16[2,16,48,768]{3,2,1,0:T(8,128)(2,1)}) async-done(((bf16[2,16,48,768]{3,2,1,0:T(8,128)(2,1)}, bf16[2,16,48,768]{3,2,1,0:T(8,128)(2,1)}), (bf16[2,16,48,768]{3,2,1,0:T(8,128)(2,1)}, bf16[2,16,48,768]{3,2,1,0:T(8,128)(2,1)})) %all-reduce.5.cloned.1.call-update) | async-done | bytes 4718608
  443.1 2.0 convert_reduce_fusion.5
  445.1 2.1 copy.79
  447.2 1.9 constant_dynamic-slice_fusion.1
  449.1 2.1 copy.78
  451.3 3.7 multiply_reduce_fusion.3
  455.2 3.9 convolution_convert_fusion.2
  459.9 102.0 %reduce_grads.1 = (bf16[96,2304]{1,0:T(8,128)(2,1)}, bf16[96,768]{1,0:T(8,128)(2,1)}, bf16[96,3072]{1,0:T(8,128)(2,1)}, bf16[384,768]{1,0:T(8,128)(2,1)}, bf16[96,1024]{1,0:T(8,128)(2,1)}, /*index=5*/f32[96,128]{1,0:T(8,128)}) custom-call(bf16[4,2,96,2304]{3,2,1,0:T(8,128)(2,1)} %bitcast.133, bf16[4,2,96,768]{3,2,1,0:T(8,128)(2,1)} %bitcast.132, ...), custom_call_target="tpu_custom_call" | custom-call | tf_op jit(solution)/shard_map/reduce_grads/pallas_call | solution.py:238
  566.0 2.2 convert_element_type.215
  568.3 2.3 convert_element_type.216
  (219 shorter events, 33.3 us)
Async XLA Ops:
  7.2 4.4 copy-start
  7.2 62.0 %all-gather.5.cloned.1.call-start = ((), (), s32[]{:S(2)}) async-start(), calls=%async_computation.1 | async-start | bytes 2949120 | tf_op jit(solution)/shard_map/all_gather | solution.py:355
  11.6 4.3 copy-start.46
  11.6 4.3 copy-start.47
  15.9 104.8 %all-gather.3.cloned.1.call-start = ((), (), s32[]{:S(2)}) async-start(), calls=%async_computation | async-start | bytes 2949120 | tf_op jit(solution)/shard_map/all_gather | solution.py:356
  18.8 7.0 %copy-start.29 = (s32[2,16,48]{2,1,0:T(8,128)S(1)}, s32[2,16,48]{2,1,0:T(8,128)}, u32[]{:S(2)}) copy-start(s32[2,16,48]{2,1,0:T(8,128)} %param.24) | copy-start | bytes 18436
  18.8 424.3 %all-reduce.5.cloned.1.call-start = ((), (), s32[]{:S(2)}) async-start(), calls=%async_computation.2 | async-start | bytes 9437184
  156.8 4.9 copy-start.59
  161.7 16.5 %slice-start.4 = ((s8[4718592]{0:T(1024)(128)(4,1)}), s8[4194304]{0:T(1024)(128)(4,1)S(1)}, s32[]{:S(2)}) async-start(s8[4718592]{0:T(1024)(128)(4,1)} %bitcast.142), calls=%async_computation.7 | async-start | bytes 8388608
  164.2 27.5 %copy-start.5 = (f32[384,768]{1,0:T(8,128)}, f32[384,768]{1,0:T(8,128)S(1)}, u32[]{:S(2)}) copy-start(f32[384,768]{1,0:T(8,128)S(1)} %get-tuple-element.68) | copy-start | bytes 3538948
  164.5 27.1 %copy-start.42 = (f32[384]{0:T(512)}, f32[384]{0:T(512)S(1)}, u32[]{:S(2)}) copy-start(f32[384]{0:T(512)S(1)} %add_rsqrt_fusion.2) | copy-start | bytes 4612
  164.5 13.7 %slice-start.5 = ((s8[4718592]{0:T(1024)(128)(4,1)}), s8[524288]{0:T(1024)(128)(4,1)S(1)}, s32[]{:S(2)}) async-start(s8[4718592]{0:T(1024)(128)(4,1)} %bitcast.142), calls=%async_computation.8 | async-start | bytes 1048576
  164.5 13.6 %copy-start.60 = (f32[768]{0:T(1024)S(1)}, f32[768]{0:T(1024)}, u32[]{:S(2)}) copy-start(f32[768]{0:T(1024)} %param.37) | copy-start | bytes 9220
  182.4 6.4 %slice-start.6 = ((s8[4718592]{0:T(1024)(128)(4,1)}), s8[4194304]{0:T(1024)(128)(4,1)S(1)}, s32[]{:S(2)}) async-start(s8[4718592]{0:T(1024)(128)(4,1)} %bitcast.144), calls=%async_computation.9 | async-start | bytes 8388608
  184.4 7.3 %copy-start.9 = (f32[384,768]{1,0:T(8,128)}, f32[384,768]{1,0:T(8,128)S(1)}, u32[]{:S(2)}) copy-start(f32[384,768]{1,0:T(8,128)S(1)} %get-tuple-element.47) | copy-start | bytes 3538948
  184.4 4.4 slice-start.7
  200.9 13.8 %copy-start.16 = (bf16[2,192,12,64]{1,3,2,0:T(8,128)(2,1)S(1)}, bf16[2,192,12,64]{1,3,2,0:T(8,128)(2,1)}, u32[]{:S(2)}) copy-start(bf16[2,192,12,64]{1,3,2,0:T(8,128)(2,1)} %copy.70) | copy-start | bytes 1769476
  200.9 13.8 %copy-start.28 = (f32[2,12,192]{2,1,0:T(8,128)S(1)}, f32[2,12,192]{2,1,0:T(8,128)}, u32[]{:S(2)}) copy-start(f32[2,12,192]{2,1,0:T(8,128)} %get-tuple-element.65) | copy-start | bytes 55300
  200.9 22.1 %slice-start = ((s8[14155776]{0:T(1024)(128)(4,1)}), s8[1572864]{0:T(1024)(128)(4,1)S(1)}, s32[]{:S(2)}) async-start(s8[14155776]{0:T(1024)(128)(4,1)} %bitcast.127), calls=%async_computation.3 | async-start | bytes 3145728
  200.9 22.1 %slice-start.1 = ((s8[14155776]{0:T(1024)(128)(4,1)}), s8[4194304]{0:T(1024)(128)(4,1)S(1)}, s32[]{:S(2)}) async-start(s8[14155776]{0:T(1024)(128)(4,1)} %bitcast.127), calls=%async_computation.4 | async-start | bytes 8388608
  200.9 22.1 %slice-start.2 = ((s8[14155776]{0:T(1024)(128)(4,1)}), s8[4194304]{0:T(1024)(128)(4,1)S(1)}, s32[]{:S(2)}) async-start(s8[14155776]{0:T(1024)(128)(4,1)} %bitcast.127), calls=%async_computation.5 | async-start | bytes 8388608
  214.7 8.3 %slice-start.3 = ((s8[14155776]{0:T(1024)(128)(4,1)}), s8[4194304]{0:T(1024)(128)(4,1)S(1)}, s32[]{:S(2)}) async-start(s8[14155776]{0:T(1024)(128)(4,1)} %bitcast.127), calls=%async_computation.6 | async-start | bytes 8388608
  223.0 9.5 %copy-start.11 = (bf16[2,192,12,64]{1,3,2,0:T(8,128)(2,1)S(1)}, bf16[2,192,12,64]{1,3,2,0:T(8,128)(2,1)}, u32[]{:S(2)}) copy-start(bf16[2,192,12,64]{1,3,2,0:T(8,128)(2,1)} %copy.65) | copy-start | bytes 1769476
  296.8 4.4 copy-start.6
  296.8 4.4 copy-start.43
  296.8 4.4 copy-start.49
  296.8 4.4 copy-start.64
  296.8 4.4 copy-start.69
  443.1 8.2 %copy-start.31 = (f32[384]{0:T(512)S(1)}, f32[384]{0:T(512)}, u32[]{:S(2)}) copy-start(f32[384]{0:T(512)} %copy-done.30) | copy-start | bytes 4612
  443.1 8.2 %copy-start.33 = (f32[384]{0:T(512)S(1)}, f32[384]{0:T(512)}, u32[]{:S(2)}) copy-start(f32[384]{0:T(512)} %copy-done.32) | copy-start | bytes 4612
  443.1 8.2 %copy-start.39 = (f32[768]{0:T(1024)S(1)}, f32[768]{0:T(1024)}, u32[]{:S(2)}) copy-start(f32[768]{0:T(1024)} %param.25) | copy-start | bytes 9220
  451.2 3.8 copy-start.18
  451.3 3.8 copy-start.19
  455.0 4.0 copy-start.26
  455.1 4.0 copy-start.38
  455.1 4.1 copy-start.36
  455.1 4.1 copy-start.53
  455.1 4.1 copy-start.52
  455.1 4.1 copy-start.41
  455.1 4.1 copy-start.40
  455.1 4.1 copy-start.51
  455.1 4.1 copy-start.50
  455.2 4.1 copy-start.37
  561.9 8.6 %copy-start.23 = (bf16[96,2304]{1,0:T(8,128)(2,1)S(1)}, bf16[96,2304]{1,0:T(8,128)(2,1)}, u32[]{:S(2)}) copy-start(bf16[96,2304]{1,0:T(8,128)(2,1)} %get-tuple-element.27) | copy-start | bytes 1327108
  566.0 5.5 copy-start.24
  566.0 6.3 %copy-start.25 = (bf16[96,768]{1,0:T(8,128)(2,1)S(1)}, bf16[96,768]{1,0:T(8,128)(2,1)}, u32[]{:S(2)}) copy-start(bf16[96,768]{1,0:T(8,128)(2,1)} %get-tuple-element.28) | copy-start | bytes 442372
  568.3 4.8 copy-start.3
  568.3 4.8 copy-start.4
  (33 other events, 83.0 us)
Sparse Core Ops, SparseCore 0:
  16.0 53.2 all-gather.4
  71.4 49.2 all-gather.2
  271.9 171.1 all-reduce.4

commit v2 on v0

--- a/solution.py
+++ b/solution.py
@@ -3,6 +3,8 @@
 import jax
 import jax.numpy as jnp
 from jax import lax
+from jax.experimental import pallas as pl
+from jax.experimental.pallas import tpu as pltpu
 from jax.sharding import PartitionSpec as P
 
 HEADS = 12
@@ -11,6 +13,1117 @@
 EPSILON = 1e-06
 SQRT_HALF = 0.7071067811865476
 INV_ROOT_TAU = 0.3989422804014327
+MESH = pl.DeviceIdType.MESH
+GRID = (8, 4)
+
+
+NT = (((1,), (1,)), ((), ()))
+TN = (((0,), (0,)), ((), ()))
+CHUNKS = 2
+
+
+def dot(left, right, dims=(((1,), (0,)), ((), ()))):
+    return lax.dot_general(left, right, dims, preferred_element_type=jnp.float32)
+
+
+def remote_copy(src, dst, send, recv, device):
+    return pltpu.make_async_remote_copy(
+        src_ref=src, dst_ref=dst, send_sem=send, recv_sem=recv, device_id=device, device_id_type=MESH
+    )
+
+
+def line_barrier(dp, z):
+    barrier = pltpu.get_barrier_semaphore()
+    for away in range(1, 4):
+        pl.semaphore_signal(
+            barrier, inc=1, device_id=(dp, lax.rem(z + away, 4)), device_id_type=MESH
+        )
+    pl.semaphore_wait(barrier, 3)
+
+
+N1_GAIN, N1_BIAS, Q_BIAS, V_BIAS, OUT_BIAS, N2_GAIN, N2_BIAS, DOWN_BIAS, N3_GAIN, N3_BIAS, UP_BIAS, ALIGN_BIAS = (
+    0, 1, 2, 3, 4, 5, 6, 7, 8, 9, 10, 14,
+)
+PACK_ROWS = 16
+TILE = 512
+
+
+def row_of(pack, row, start, size):
+    width = pack.shape[1]
+    parts = []
+    while size > 0:
+        line, column = row + start // width, start % width
+        take = min(size, width - column)
+        parts.append(pack[line : line + 1, column : column + take])
+        start, size = start + take, size - take
+    return parts[0] if len(parts) == 1 else jnp.concatenate(parts, axis=1)
+
+
+def norm_rows(values):
+    center = values - jnp.mean(values, axis=-1, keepdims=True)
+    inverse = lax.rsqrt(jnp.mean(center * center, axis=-1, keepdims=True) + EPSILON)
+    return center * inverse, inverse
+
+
+def feed_kernel(
+    tok, att, vis, pack, w_out, w_up, w_down, w_align,
+    block_out, align_out, act_t, slope, unit2, inv2, unit3, inv3, normed2_t, normed3_t, att_t,
+    out_v, up_v, down_v, align_v, attended, mid, normed, hidden, act, slope_v, act_tv, trans, w_sem, put_sem,
+):
+    rows, width = tok.shape
+    wide = up_v.shape[1]
+    half = width // 2
+    weights = [
+        pltpu.make_async_copy(src, dst, w_sem.at[k])
+        for k, (src, dst) in enumerate(((w_out, out_v), (w_up, up_v), (w_down, down_v), (w_align, align_v)))
+    ]
+    for copy in weights:
+        copy.start()
+    chunk = 32
+
+    def transposed(k, source, target):
+        for c in range(0, width, 128):
+            trans[k, pl.ds(c, 128), :] = source[:, pl.ds(c, 128)].T
+        copy = pltpu.make_async_copy(trans.at[k], target, put_sem.at[k])
+        copy.start()
+        return copy
+
+    for c in range(2):
+        for h in range(2):
+            attended[pl.ds(c * rows // 2, rows // 2), pl.ds(h * half, half)] = att[c, h]
+    puts = [transposed(0, attended, att_t)]
+    weights[0].wait()
+    for c in range(0, width, 256):
+        at = pl.ds(c, 256)
+        mid[:, at] = (
+            tok[:, at].astype(jnp.float32) + dot(attended[...], out_v[:, at]) + pack[OUT_BIAS : OUT_BIAS + 1, at]
+        )
+
+    def norm(gain, bias, unit, inv):
+        def body(k, _):
+            at = pl.ds(pl.multiple_of(k * chunk, chunk), chunk)
+            one, inverse = norm_rows(mid[at, :])
+            unit[at, :] = one.astype(jnp.bfloat16)
+            inv[at, :] = inverse
+            normed[at, :] = (one * pack[gain : gain + 1, :] + pack[bias : bias + 1, :]).astype(jnp.bfloat16)
+            return 0
+
+        lax.fori_loop(0, rows // chunk, body, 0)
+
+    norm(N2_GAIN, N2_BIAS, unit2, inv2)
+    puts.append(transposed(1, normed, normed2_t))
+    weights[1].wait()
+    for t in range(wide // TILE):
+        at = pl.ds(t * TILE, TILE)
+        hidden[...] = dot(normed[...], up_v[:, at]) + row_of(pack, UP_BIAS, t * TILE, TILE)
+
+        def body(k, _):
+            here = pl.ds(pl.multiple_of(k * chunk, chunk), chunk)
+            values = hidden[here, :]
+            cdf = 0.5 * (1.0 + lax.erf(values * SQRT_HALF))
+            act[here, at] = (values * cdf).astype(jnp.bfloat16)
+            slope_v[here, at] = (
+                cdf + values * jnp.exp(-0.5 * values * values) * INV_ROOT_TAU
+            ).astype(jnp.bfloat16)
+            return 0
+
+        lax.fori_loop(0, rows // chunk, body, 0)
+        for c in range(0, TILE, 128):
+            act_tv[pl.ds(t * TILE + c, 128), :] = act[:, pl.ds(t * TILE + c, 128)].T
+        copy = pltpu.make_async_copy(act_tv.at[pl.ds(t * TILE, TILE)], act_t.at[pl.ds(t * TILE, TILE)], put_sem.at[4 + t])
+        copy.start()
+        puts.append(copy)
+    copy = pltpu.make_async_copy(slope_v, slope, put_sem.at[3])
+    copy.start()
+    puts.append(copy)
+    weights[2].wait()
+    for c in range(0, width, 256):
+        at = pl.ds(c, 256)
+        mid[:, at] = mid[:, at] + dot(act[...], down_v[:, at]) + pack[DOWN_BIAS : DOWN_BIAS + 1, at]
+    block_out[...] = (vis[...] * mid[...]).astype(jnp.bfloat16)
+    norm(N3_GAIN, N3_BIAS, unit3, inv3)
+    puts.append(transposed(2, normed, normed3_t))
+    weights[3].wait()
+    for c in range(0, align_v.shape[1], 256):
+        at = pl.ds(c, 256)
+        target = dot(normed[...], align_v[:, at]) + row_of(pack, ALIGN_BIAS, c, 256)
+        align_out[:, at] = (vis[...] * target).astype(jnp.bfloat16)
+    for copy in puts:
+        copy.wait()
+
+
+def feed(tok, att, vis, pack, w_out, w_up, w_down, w_align):
+    rows, width = tok.shape
+    wide, align = w_up.shape[1], w_align.shape[1]
+    vmem = pl.BlockSpec(memory_space=pltpu.VMEM)
+    hbm = pl.BlockSpec(memory_space=pl.ANY)
+    low = jnp.bfloat16
+    struct = jax.ShapeDtypeStruct
+    return pl.pallas_call(
+        feed_kernel,
+        name="feed",
+        out_shape=[
+            struct((rows, width), low),
+            struct((rows, align), low),
+            struct((wide, rows), low),
+            struct((rows, wide), low),
+            struct((rows, width), low),
+            struct((rows, 1), jnp.float32),
+            struct((rows, width), low),
+            struct((rows, 1), jnp.float32),
+            struct((width, rows), low),
+            struct((width, rows), low),
+            struct((width, rows), low),
+        ],
+        in_specs=[vmem] * 4 + [hbm] * 4,
+        out_specs=[vmem, vmem, hbm, hbm, vmem, vmem, vmem, vmem, hbm, hbm, hbm],
+        scratch_shapes=[
+            pltpu.VMEM(w_out.shape, low),
+            pltpu.VMEM(w_up.shape, low),
+            pltpu.VMEM(w_down.shape, low),
+            pltpu.VMEM(w_align.shape, low),
+            pltpu.VMEM((rows, width), low),
+            pltpu.VMEM((rows, width), jnp.float32),
+            pltpu.VMEM((rows, width), low),
+            pltpu.VMEM((rows, TILE), jnp.float32),
+            pltpu.VMEM((rows, wide), low),
+            pltpu.VMEM((rows, wide), low),
+            pltpu.VMEM((wide, rows), low),
+            pltpu.VMEM((3, width, rows), low),
+            pltpu.SemaphoreType.DMA((4,)),
+            pltpu.SemaphoreType.DMA((4 + wide // TILE,)),
+        ],
+        compiler_params=pltpu.CompilerParams(vmem_limit_bytes=56 * 2**20),
+    )(tok, att, vis, pack, w_out, w_up, w_down, w_align)
+
+
+def attend_kernel(
+    tok, pack, w_hbm, key_bias,
+    att, n1, unit, qkv, own_att, lse,
+    xall, w_low, w_sem, pair_send, cross_send, fwd_send, recv, att_send, att_recv,
+):
+    dp = lax.axis_index("dp")
+    z = lax.axis_index("blk")
+    clip, side = z // 2, lax.rem(z, 2)
+    rows, width = tok.shape[1], tok.shape[2]
+    half = width // 2
+    partner = z + 1 - 2 * side
+    is_mid = (z == 1) | (z == 2)
+    other_mid = 2 - clip
+    near, far = 3 - z, lax.rem(z + 2, 4)
+    columns = pl.ds(pl.multiple_of(side * half, 128), half)
+
+    def w_copy(m):
+        start = pl.multiple_of(m * width + side * half, 128)
+        return pltpu.make_async_copy(w_hbm.at[:, pl.ds(start, half)], w_low.at[m], w_sem.at[m])
+
+    for m in range(3):
+        w_copy(m).start()
+    line_barrier(dp, z)
+    step = rows // CHUNKS
+
+    def cross_copy(k):
+        at = pl.ds(k * step, step)
+        return remote_copy(
+            tok.at[1 - clip, at], xall.at[z, at], cross_send.at[k], recv.at[z, k], (dp, other_mid)
+        )
+
+    def pair_copy(k):
+        at = pl.ds(k * step, step)
+        return remote_copy(
+            tok.at[clip, at], xall.at[z, at], pair_send.at[k], recv.at[z, k], (dp, partner)
+        )
+
+    def arrival(slot, k):
+        at = pl.ds(k * step, step)
+        return remote_copy(
+            tok.at[clip, at], xall.at[slot, at], pair_send.at[k], recv.at[slot, k], (dp, partner)
+        )
+
+    def forward_copy(slot, which, k):
+        at = pl.ds(k * step, step)
+        return remote_copy(
+            xall.at[slot, at], xall.at[slot, at], fwd_send.at[which, k], recv.at[slot, k], (dp, partner)
+        )
+
+    for k in range(CHUNKS):
+        cross_copy(k).start()
+    for k in range(CHUNKS):
+        pair_copy(k).start()
+    xall[z] = tok[clip]
+    for m in range(3):
+        w_copy(m).wait()
+
+    def project(slot):
+        for k in range(rows // 32):
+            at = pl.ds(k * 32, 32)
+            values = xall[slot, at, :].astype(jnp.float32)
+            one, _ = norm_rows(values)
+            unit[slot, at, :] = one.astype(jnp.bfloat16)
+            n1[slot, at, :] = (
+                one * pack[N1_GAIN : N1_GAIN + 1, :] + pack[N1_BIAS : N1_BIAS + 1, :]
+            ).astype(jnp.bfloat16)
+        where = pl.ds(pl.multiple_of(slot * rows, rows), rows)
+        normed = n1[slot]
+        qkv[0, where, :] = (
+            (dot(normed, w_low[0]) + pack[Q_BIAS : Q_BIAS + 1, columns]).astype(jnp.bfloat16)
+            * jnp.bfloat16(0.125)
+        )
+        qkv[1, where, :] = dot(normed, w_low[1]).astype(jnp.bfloat16)
+        qkv[2, where, :] = (
+            dot(normed, w_low[2]) + pack[V_BIAS : V_BIAS + 1, columns]
+        ).astype(jnp.bfloat16)
+
+    project(z)
+
+    @pl.when(is_mid)
+    def _():
+        for k in range(CHUNKS):
+            for which, slot in enumerate((near, far)):
+                arrival(slot, k).wait_recv()
+                forward_copy(slot, which, k).start()
+        for k in range(CHUNKS):
+            arrival(partner, k).wait_recv()
+
+    def later(number, _):
+        slot = jnp.where(number == 0, partner, jnp.where(number == 1, jnp.where(is_mid, near, far), jnp.where(is_mid, far, near)))
+
+        @pl.when(jnp.logical_not(is_mid))
+        def _():
+            for k in range(CHUNKS):
+                arrival(slot, k).wait_recv()
+
+        project(slot)
+        return 0
+
+    lax.fori_loop(0, 3, later, 0)
+
+    lane = lax.broadcasted_iota(jnp.int32, (1, 128), 1)
+    low_lane = lane < 64
+
+    def att_copy(slot):
+        return remote_copy(
+            own_att.at[slot], att.at[clip, side], att_send.at[slot], att_recv.at[z], (dp, slot)
+        )
+
+    def piece(number, _):
+        slot = jnp.where(number == 0, far, jnp.where(number == 1, near, jnp.where(number == 2, partner, z)))
+        where = pl.ds(pl.multiple_of(slot * rows, rows), rows)
+        stats = jnp.zeros((rows, 128), jnp.float32)
+        for t in range(half // 128):
+            at = pl.ds(t * 128, 128)
+            queries = qkv[0, where, at]
+            keys = qkv[1, :, at]
+            values = qkv[2, :, at]
+            parts = []
+            for a in range(2):
+                mine = low_lane if a == 0 else jnp.logical_not(low_lane)
+                masked = jnp.where(mine, queries, jnp.zeros_like(queries))
+                scores = dot(masked, keys, NT) + key_bias[...]
+                top = jnp.max(scores, axis=-1, keepdims=True)
+                expo = jnp.exp(scores - top)
+                total = jnp.sum(expo, axis=-1, keepdims=True)
+                parts.append(dot(expo.astype(jnp.bfloat16), values) * (1.0 / total))
+                stats = jnp.where(lane == 2 * t + a, top + jnp.log(total), stats)
+            own_att[slot, :, at] = jnp.where(low_lane, parts[0], parts[1]).astype(jnp.bfloat16)
+        lse[where, :] = stats
+
+        @pl.when(number < 3)
+        def _():
+            att_copy(slot).start()
+
+        return 0
+
+    lax.fori_loop(0, 4, piece, 0)
+    att[clip, side] = own_att[z]
+
+    def settle(number, _):
+        slot = lax.rem(z + number, 4)
+        att_copy(slot).wait_send()
+        remote_copy(
+            own_att.at[slot], att.at[slot // 2, lax.rem(slot, 2)], att_send.at[slot], att_recv.at[slot], (dp, slot)
+        ).wait_recv()
+        return 0
+
+    lax.fori_loop(1, 4, settle, 0)
+    for k in range(CHUNKS):
+        cross_copy(k).wait_send()
+        pair_copy(k).wait_send()
+
+    @pl.when(is_mid)
+    def _():
+        for k in range(CHUNKS):
+            for which, slot in enumerate((near, far)):
+                forward_copy(slot, which, k).wait_send()
+
+
+def attend(tokens, pack, w_qkv, key_bias):
+    clips, rows, width = tokens.shape
+    half = width // 2
+    vmem = pl.BlockSpec(memory_space=pltpu.VMEM)
+    dma = pltpu.SemaphoreType.DMA
+    low = jnp.bfloat16
+    return pl.pallas_call(
+        attend_kernel,
+        name="attend",
+        out_shape=[
+            jax.ShapeDtypeStruct((2, 2, rows, half), low),
+            jax.ShapeDtypeStruct((4, rows, width), low),
+            jax.ShapeDtypeStruct((4, rows, width), low),
+            jax.ShapeDtypeStruct((3, 4 * rows, half), low),
+            jax.ShapeDtypeStruct((4, rows, half), low),
+            jax.ShapeDtypeStruct((4 * rows, 128), jnp.float32),
+        ],
+        in_specs=[vmem, vmem, pl.BlockSpec(memory_space=pl.ANY), vmem],
+        out_specs=[vmem] * 6,
+        scratch_shapes=[
+            pltpu.VMEM((4, rows, width), low),
+            pltpu.VMEM((3, width, half), low),
+            dma((3,)),
+            dma((CHUNKS,)),
+            dma((CHUNKS,)),
+            dma((2, CHUNKS)),
+            dma((4, CHUNKS)),
+            dma((4,)),
+            dma((4,)),
+        ],
+        compiler_params=pltpu.CompilerParams(
+            collective_id=1, has_side_effects=True, vmem_limit_bytes=56 * 2**20
+        ),
+    )(tokens, pack, w_qkv, key_bias)
+
+
+KEY_BLOCK = 256
+
+
+JOBS = (
+    (4, 0, 96, 0, 1024, 0),
+    (3, 0, 192, 0, 768, 2),
+    (3, 192, 192, 0, 768, 2),
+    (2, 0, 96, 0, 1536, 0),
+    (2, 0, 96, 1536, 1536, 1),
+    (1, 0, 96, 0, 768, 0),
+    (0, 0, 96, 0, 1152, 1),
+)
+ALIGN, DOWN0, DOWN1, UP0, UP1, OUT, QKV = range(7)
+COUNT = len(JOBS)
+SEND_SHAPES = ((2, 2, 2, 48, 1536), (2, 2, 2, 48, 1536), (2, 2, 2, 96, 768))
+
+
+def add_into(target, first, second):
+    rows = target.shape[-2]
+    step = 48 if rows % 48 == 0 else 32
+
+    def body(k, _):
+        at = pl.ds(pl.multiple_of(k * step, step), step)
+        target[..., at, :] = (
+            first[..., at, :].astype(jnp.float32) + second[..., at, :].astype(jnp.float32)
+        ).astype(target.dtype)
+        return 0
+
+    lax.fori_loop(0, rows // step, body, 0)
+
+
+LOADS = (
+    "cot_a", "l3", "align", "unit3", "cot_b", "down", "slope", "ld", "up", "unit2", "out", "l2", "la",
+    "n1", "lse", "own_att", "qkv0", "qkv1", "qkv2", "unit1", "low0", "low1", "low2",
+    "l3_far", "ld_far", "l2_far", "la_far",
+)
+
+
+def back_kernel(*refs):
+    (
+        vis, pack, key_bias, inv2, inv3, tok,
+        cot_a_h, cot_b_h, unit2_h, unit3_h, slope_h, l3_h, ld_h, l2_h, la_h,
+        qkv_h, own_att_h, lse_h, n1_h, unit1_h, w_align, w_down, w_up, w_out, w_qkv,
+    ) = refs[:25]
+    grad_tokens, vec_out = refs[25:27]
+    outs = refs[27:32]
+    rest = refs[32:]
+    own, got0, got1, got2 = (rest[i * COUNT : (i + 1) * COUNT] for i in range(4))
+    rest = rest[4 * COUNT :]
+    gotz = rest[: COUNT - 1]
+    rest = rest[COUNT - 1 :]
+    (
+        gotq, send_a, send_b, send_c, vec_got,
+        align_v, down_v, up_v, out_v, cot_a, cot_b, unit2, unit3, slope, l3, ld, l2, la,
+        e_v, mid_v, low_d, low_o, in_src, grad_att, n1s, lse, lse_rows, spread_rows, grad_q,
+        from_pair, from_end, total_in,
+        load_sem, send0, recv0, send1, recv1, send2, recv2, sendz, recvz, sendq, recvq, out_sem, vsend, vrecv,
+        in_send, in_recv, pair_send, pair_recv, end_send, end_recv, out_send, out_recv,
+    ) = rest
+    buffers = (send_a, send_b, send_c)
+
+    dp = lax.axis_index("dp")
+    z = lax.axis_index("blk")
+    core = lax.rem(dp, 2)
+    x = lax.rem(dp // 2, 2)
+    y = dp // 4
+    clip, side = z // 2, lax.rem(z, 2)
+    to_core = (dp + 1 - 2 * core, z)
+    to_x = (dp + 2 - 4 * x, z)
+    to_y = (dp + 4 - 8 * y, z)
+    partner = z + 1 - 2 * side
+    to_z1 = (dp, partner)
+    to_z2 = (dp, lax.rem(z + 2, 4))
+    to_z3 = (dp, 3 - z)
+    is_mid = (z == 1) | (z == 2)
+    is_end = (z == 0) | (z == 3)
+    rows, width = tok.shape
+    half, piece = width // 2, rows // 2
+    wide = slope.shape[1]
+    low = jnp.bfloat16
+
+    def load(name, src, dst):
+        return pltpu.make_async_copy(src, dst, load_sem.at[LOADS.index(name)])
+
+    def qkv_at(m):
+        return up_v.at[:, pl.ds(m * half, half)]
+
+    def low_at(m):
+        return up_v.at[:, pl.ds((3 + m) * half, half)]
+
+    def grad_at(m):
+        return down_v.at[pl.ds((2 if m == 0 else 3) * width, width), pl.ds(half if m != 1 else 0, half)]
+
+    unit1 = down_v.at[pl.ds(0, width)]
+    n1 = down_v.at[pl.ds(width, width)]
+    own_att = down_v.at[pl.ds(2 * width, width), pl.ds(0, half)]
+
+    def e_at(slot):
+        return align_v.at[pl.ds(pl.multiple_of(slot * piece, piece), piece), pl.ds(0, width)]
+
+    def halves(name, src, dst):
+        return [
+            load(name + "_far", src.at[:, 1 - core], dst.at[0]),
+            load(name, src.at[:, core], dst.at[1]),
+        ]
+
+    first = {
+        "cot_a": [load("cot_a", cot_a_h, cot_a)],
+        "l3": halves("l3", l3_h, l3),
+        "align": [load("align", w_align, align_v)],
+        "unit3": [load("unit3", unit3_h, unit3)],
+        "cot_b": [load("cot_b", cot_b_h, cot_b)],
+        "down": [load("down", w_down, down_v)],
+        "slope": [load("slope", slope_h, slope)],
+        "ld": halves("ld", ld_h, ld),
+        "up": [load("up", w_up, up_v)],
+        "unit2": [load("unit2", unit2_h, unit2)],
+        "out": [load("out", w_out, out_v)],
+        "l2": halves("l2", l2_h, l2),
+        "la": halves("la", la_h, la),
+        "lse": [load("lse", lse_h, lse)],
+    }
+    second = {
+        "n1": [load("n1", n1_h, n1)],
+        "own_att": [load("own_att", own_att_h, own_att)],
+        "unit1": [load("unit1", unit1_h, unit1)],
+    }
+    for m in range(3):
+        second["qkv%d" % m] = [load("qkv%d" % m, qkv_h.at[m], qkv_at(m))]
+        column = pl.multiple_of(m * width + side * half, 128)
+        second["low%d" % m] = [load("low%d" % m, w_qkv.at[:, pl.ds(column, half)], low_at(m))]
+    for copies in first.values():
+        for copy in copies:
+            copy.start()
+
+    def ready(*names):
+        for name in names:
+            for copy in {**first, **second}[name]:
+                copy.wait()
+
+    barrier = pltpu.get_barrier_semaphore()
+    for device in (to_core, to_x, to_y, to_z1, to_z2, to_z3):
+        pl.semaphore_signal(barrier, inc=1, device_id=device, device_id_type=MESH)
+    pl.semaphore_wait(barrier, 6)
+
+    def copies0(j):
+        columns = JOBS[j][4]
+        for h in range(2):
+            yield remote_copy(
+                buffers[JOBS[j][5]].at[h, :, :, :, pl.ds(0, columns)], got0[j].at[h], send0.at[j, h], recv0.at[j, h], to_core
+            )
+
+    def copies1(j):
+        yield remote_copy(own[j].at[0, 1 - x], got1[j].at[0], send1.at[j, 0], recv1.at[j, 0], to_x)
+        yield remote_copy(own[j].at[1, 1 - y], got1[j].at[1], send1.at[j, 1], recv1.at[j, 1], to_y)
+
+    def copies2(j):
+        yield remote_copy(own[j].at[0, x, 1 - y], got2[j].at[0], send2.at[j, 0], recv2.at[j, 0], to_y)
+        yield remote_copy(own[j].at[1, y, 1 - x], got2[j].at[1], send2.at[j, 1], recv2.at[j, 1], to_x)
+
+    def shares(j):
+        return (own[j].at[0, x, y], own[j].at[1, y, x])
+
+    def copiesz(j, slot, device):
+        for h, share in enumerate(shares(j)):
+            yield remote_copy(share, gotz[j].at[slot, h], sendz.at[j, slot, h], recvz.at[j, slot, h], device)
+
+    def copiesq(source, slot, device):
+        for h, share in enumerate(shares(QKV)):
+            yield remote_copy(
+                share if source is None else gotq.at[source, h],
+                gotq.at[slot, h], sendq.at[slot, h], recvq.at[slot, h], device,
+            )
+
+    def result(j, h, source):
+        matrix, row, count, column, columns, _ = JOBS[j]
+        return pltpu.make_async_copy(
+            source, outs[matrix].at[pl.ds(row + h * count // 2, count // 2), pl.ds(column, columns)], out_sem.at[j, h]
+        )
+
+    def result_q(h, which, source):
+        count = JOBS[QKV][2] // 2
+        at = side if which == 0 else 1 - side
+        for m in range(3):
+            column = pl.multiple_of(m * width + at * half, 128)
+            yield pltpu.make_async_copy(
+                source.at[:, pl.ds(m * half, half)],
+                outs[0].at[pl.ds(h * count, count), pl.ds(column, half)],
+                out_sem.at[QKV + which * 3 + m, h],
+            )
+
+    def stage(j, number):
+        if number == 0:
+            for copy in copies0(j):
+                copy.start()
+        if number == 1:
+            for copy in copies0(j):
+                copy.wait()
+            add_into(own[j], own[j], got0[j])
+            for copy in copies1(j):
+                copy.start()
+        if number == 2:
+            for copy in copies1(j):
+                copy.wait()
+            add_into(own[j].at[0, x], own[j].at[0, x], got1[j].at[0])
+            add_into(own[j].at[1, y], own[j].at[1, y], got1[j].at[1])
+            for copy in copies2(j):
+                copy.start()
+        if number == 3:
+            for copy in copies2(j):
+                copy.wait()
+            for h, share in enumerate(shares(j)):
+                add_into(share, share, got2[j].at[h])
+
+            @pl.when(is_end)
+            def _():
+                for copy in copiesq(None, 0, to_z1) if j == QKV else copiesz(j, 0, to_z1):
+                    copy.start()
+
+        if number >= 4 and j == QKV:
+            stage_q(number)
+            return
+        if number == 4:
+
+            @pl.when(is_mid)
+            def _():
+                for copy in copiesz(j, 0, to_z1):
+                    copy.wait_recv()
+                for h, share in enumerate(shares(j)):
+                    add_into(share, share, gotz[j].at[0, h])
+                for copy in copiesz(j, 1, to_z3):
+                    copy.start()
+
+            @pl.when(is_end)
+            def _():
+                for copy in copiesz(j, 0, to_z1):
+                    copy.wait_send()
+
+        if number == 5:
+
+            @pl.when(is_mid)
+            def _():
+                for copy in copiesz(j, 1, to_z3):
+                    copy.wait()
+                for h, share in enumerate(shares(j)):
+                    add_into(share, share, gotz[j].at[1, h])
+                for copy in copiesz(j, 0, to_z1):
+                    copy.start()
+                for h, share in enumerate(shares(j)):
+                    result(j, h, share).start()
+
+        if number == 6:
+
+            @pl.when(is_mid)
+            def _():
+                for copy in copiesz(j, 0, to_z1):
+                    copy.wait_send()
+
+            @pl.when(is_end)
+            def _():
+                for copy in copiesz(j, 0, to_z1):
+                    copy.wait_recv()
+                for h in range(2):
+                    result(j, h, gotz[j].at[0, h]).start()
+
+            for h in range(2):
+                result(j, h, gotz[j].at[0, h]).wait()
+
+    def stage_q(number):
+        if number == 4:
+
+            @pl.when(is_mid)
+            def _():
+                for copy in copiesq(None, 1, to_z3):
+                    copy.start()
+                for copy in copiesq(None, 0, to_z1):
+                    copy.wait_recv()
+                for copy in copiesq(0, 2, to_z3):
+                    copy.start()
+
+            @pl.when(is_end)
+            def _():
+                for copy in copiesq(None, 0, to_z1):
+                    copy.wait_send()
+
+        if number == 5:
+
+            @pl.when(is_mid)
+            def _():
+                for copy in copiesq(None, 1, to_z3):
+                    copy.wait()
+                for copy in copiesq(0, 2, to_z3):
+                    copy.wait()
+                for h, share in enumerate(shares(QKV)):
+                    add_into(share, share, gotq.at[2, h])
+                    add_into(gotq.at[0, h], gotq.at[0, h], gotq.at[1, h])
+                for copy in copiesq(None, 1, to_z1):
+                    copy.start()
+                for copy in copiesq(0, 0, to_z1):
+                    copy.start()
+                for h, share in enumerate(shares(QKV)):
+                    for copy in result_q(h, 0, share):
+                        copy.start()
+                    for copy in result_q(h, 1, gotq.at[0, h]):
+                        copy.start()
+
+        if number == 6:
+
+            @pl.when(is_mid)
+            def _():
+                for copy in copiesq(None, 1, to_z1):
+                    copy.wait_send()
+                for copy in copiesq(0, 0, to_z1):
+                    copy.wait_send()
+
+            @pl.when(is_end)
+            def _():
+                for copy in copiesq(None, 1, to_z1):
+                    copy.wait_recv()
+                for copy in copiesq(0, 0, to_z1):
+                    copy.wait_recv()
+                for h in range(2):
+                    for copy in result_q(h, 0, gotq.at[0, h]):
+                        copy.start()
+                    for copy in result_q(h, 1, gotq.at[1, h]):
+                        copy.start()
+
+            for h in range(2):
+                for which in range(2):
+                    for copy in result_q(h, which, gotq.at[0, h]):
+                        copy.wait()
+
+    def tick(*pairs):
+        for j, number in pairs:
+            stage(j, number)
+
+    def gradient(j, mine, lhs, rhs):
+        _, row, count, column, columns, buffer = JOBS[j]
+        target = own[j] if mine else buffers[buffer]
+        left = lhs[1 if mine else 0, :, pl.ds(row, count), :].reshape(4 * count, lhs.shape[3])
+        step = 512 if columns % 512 == 0 else 384
+        for c in range(0, columns, step):
+            right = rhs(c) if callable(rhs) else rhs[:, pl.ds(column + c, step)]
+            value = dot(left, right).astype(low)
+            for chip in range(4):
+                cy, cx = chip // 2, chip % 2
+                for h in range(2):
+                    i, k = (cx, cy) if h == 0 else (cy, cx)
+                    start = chip * count + h * count // 2
+                    target[h, i, k, :, pl.ds(c, step)] = value[start : start + count // 2]
+
+    def both(j, lhs, rhs):
+        gradient(j, False, lhs, rhs)
+        stage(j, 0)
+        gradient(j, True, lhs, rhs)
+
+    def put_vector(row, start, value):
+        at = 0
+        while at < value.shape[1]:
+            line, column = row + (start + at) // width, (start + at) % width
+            take = min(value.shape[1] - at, width - column)
+            vec_out[line : line + 1, column : column + take] = value[:, at : at + take]
+            at += take
+
+    def total(value):
+        return jnp.sum(value.astype(jnp.float32), axis=0, keepdims=True)
+
+    chunk = 32
+
+    def chunks(body, carry):
+        def step(k, carry):
+            return body(pl.ds(pl.multiple_of(k * chunk, chunk), chunk), carry)
+
+        return lax.fori_loop(0, rows // chunk, step, carry)
+
+    zero_row = jnp.zeros((1, width), jnp.float32)
+
+    def norm_back(e, one, inverse, gain):
+        scaled = e * gain
+        return inverse * (
+            scaled
+            - jnp.mean(scaled, axis=-1, keepdims=True)
+            - one * jnp.mean(scaled * one, axis=-1, keepdims=True)
+        )
+
+    def norm_pass(unit, inv, gain_row, base, target, low_target, sums):
+        def body(at, carry):
+            e = e_v[at, :]
+            one = unit[at, :].astype(jnp.float32)
+            value = base(at) + norm_back(e, one, inv[at, :], pack[gain_row : gain_row + 1, :])
+            target[at, :] = value
+            rounded = value.astype(low)
+            low_target[at, :] = rounded
+            return (carry[0] + total(e * one), carry[1] + total(e), carry[2] + total(rounded))
+
+        for row, value in zip(sums, chunks(body, (zero_row,) * 3)):
+            put_vector(row, 0, value)
+
+    vec_out[...] = jnp.zeros_like(vec_out)
+    ready("cot_a")
+
+    def mask(at, carry):
+        value = (vis[at, :] * cot_a[at, :].astype(jnp.float32)).astype(low)
+        cot_a[at, :] = value
+        return carry + total(value)
+
+    put_vector(ALIGN_BIAS, 0, chunks(mask, jnp.zeros((1, cot_a.shape[1]), jnp.float32)))
+    ready("l3")
+    both(ALIGN, l3, cot_a)
+    ready("align")
+    for c in range(0, width, 256):
+        e_v[:, pl.ds(c, 256)] = dot(cot_a[...], align_v[pl.ds(c, 256), :], NT)
+    tick((ALIGN, 1))
+    ready("unit3", "cot_b")
+    norm_pass(
+        unit3, inv3, N3_GAIN, lambda at: vis[at, :] * cot_b[at, :].astype(jnp.float32), mid_v, low_d,
+        (N3_GAIN, N3_BIAS, DOWN_BIAS),
+    )
+
+    ready("down", "slope")
+    for c in range(0, wide, TILE):
+        at = pl.ds(c, TILE)
+        value = (dot(low_d[...], down_v[at, :], NT) * slope[:, at].astype(jnp.float32)).astype(low)
+        slope[:, at] = value
+        put_vector(UP_BIAS, c, total(value))
+    ready("ld")
+    both(DOWN0, ld, low_d)
+    tick((ALIGN, 2), (DOWN0, 1))
+    both(DOWN1, ld, low_d)
+    for name in ("n1", "own_att", "unit1"):
+        for copy in second[name]:
+            copy.start()
+    ready("up")
+    for c in range(0, width, 256):
+        e_v[:, pl.ds(c, 256)] = dot(slope[...], up_v[pl.ds(c, 256), :], NT)
+    for m in range(3):
+        for name in ("qkv%d" % m, "low%d" % m):
+            for copy in second[name]:
+                copy.start()
+    ready("unit2")
+    norm_pass(
+        unit2, inv2, N2_GAIN, lambda at: mid_v[at, :], mid_v, low_o, (N2_GAIN, N2_BIAS, OUT_BIAS)
+    )
+    ready("out")
+    for h in range(2):
+        value = dot(low_o[...], out_v[pl.ds(h * half, half), :], NT).astype(low)
+        for c in range(2):
+            in_src[c, h] = value[c * piece : (c + 1) * piece]
+
+    def in_copy(slot):
+        return remote_copy(
+            in_src.at[slot // 2, lax.rem(slot, 2)], grad_att.at[z], in_send.at[slot], in_recv.at[z], (dp, slot)
+        )
+
+    def start_in(number, _):
+        in_copy(lax.rem(z + number, 4)).start()
+        return 0
+
+    lax.fori_loop(1, 4, start_in, 0)
+    grad_att[z] = in_src[clip, side]
+    tick((ALIGN, 3), (DOWN0, 2), (DOWN1, 1))
+    ready("l2")
+    both(UP0, l2, slope)
+    both(UP1, l2, slope)
+    ready("n1", "lse")
+    for c in range(0, width, 128):
+        flipped = n1[:, pl.ds(c, 128)].T
+        at = 0
+        while at < 128:
+            share, inside = (c + at) // 96, (c + at) % 96
+            take = min(128 - at, 96 - inside)
+            n1s[share % 2, share // 2, pl.ds(inside, take), :] = flipped[at : at + take]
+            at += take
+    lse_rows[...] = lse[...].T[:8]
+    tick((ALIGN, 4), (DOWN0, 3), (DOWN1, 2), (UP0, 1))
+    ready("la")
+    both(OUT, la, low_o)
+
+    def settle(number, _):
+        slot = lax.rem(z + number, 4)
+        in_copy(slot).wait_send()
+        remote_copy(
+            in_src.at[0, 0], grad_att.at[slot], in_send.at[slot], in_recv.at[slot], (dp, slot)
+        ).wait_recv()
+        return 0
+
+    lax.fori_loop(1, 4, settle, 0)
+    ready("own_att", "qkv0", "qkv1", "qkv2")
+    lane = lax.broadcasted_iota(jnp.int32, (1, 128), 1)
+    low_lane = lane < 64
+
+    def spread_of(slot, _):
+        where = pl.ds(pl.multiple_of(slot * piece, piece), piece)
+        stats = jnp.zeros((piece, 128), jnp.float32)
+        for t in range(half // 128):
+            at = pl.ds(t * 128, 128)
+            product = grad_att[slot, :, at].astype(jnp.float32) * own_att[where, at].astype(jnp.float32)
+            for a in range(2):
+                mine = low_lane if a == 0 else jnp.logical_not(low_lane)
+                value = jnp.sum(jnp.where(mine, product, 0.0), axis=-1, keepdims=True)
+                stats = jnp.where(lane == 2 * t + a, value, stats)
+        lse[where, :] = stats
+        return 0
+
+    lax.fori_loop(0, 4, spread_of, 0)
+    spread_rows[...] = lse[...].T[:8]
+    q_ref, k_ref, v_ref = (qkv_at(m) for m in range(3))
+    gq_ref, gk_ref, gv_ref = (grad_at(m) for m in range(3))
+
+    def pair(t):
+        at = pl.ds(t * 128, 128)
+        grad_q[...] = jnp.zeros_like(grad_q)
+        queries = q_ref[:, at]
+        grads = grad_att[:, :, at].reshape(4 * piece, 128)
+
+        def block(b, _):
+            keys_at = pl.ds(pl.multiple_of(b * KEY_BLOCK, KEY_BLOCK), KEY_BLOCK)
+            keys = k_ref[keys_at, at]
+            values = v_ref[keys_at, at]
+            grad_k = jnp.zeros((KEY_BLOCK, 128), jnp.float32)
+            grad_v = jnp.zeros((KEY_BLOCK, 128), jnp.float32)
+            grad_queries = grad_q[...]
+            for a in range(2):
+                mine = low_lane if a == 0 else jnp.logical_not(low_lane)
+                zero = jnp.zeros((), low)
+                q_mine = jnp.where(mine, queries, zero)
+                g_mine = jnp.where(mine, grads, zero)
+                k_mine = jnp.where(mine, keys, zero)
+                row = pl.ds(2 * t + a, 1)
+                scores = dot(keys, q_mine, NT) + key_bias[keys_at, :]
+                probs = jnp.exp(scores - lse_rows[row, :])
+                back = probs * (dot(values, g_mine, NT) - spread_rows[row, :])
+                back = back.astype(low)
+                grad_v = grad_v + dot(probs.astype(low), g_mine)
+                grad_k = grad_k + dot(back, q_mine)
+                grad_queries = grad_queries + dot(back, k_mine, TN)
+            grad_q[...] = grad_queries
+            gk_ref[keys_at, at] = grad_k.astype(low)
+            gv_ref[keys_at, at] = grad_v.astype(low)
+            return 0
+
+        lax.fori_loop(0, 4 * piece // KEY_BLOCK, block, 0)
+        gq_ref[:, at] = (grad_q[...] * 0.125).astype(low)
+
+    pair(0)
+    tick((ALIGN, 5), (DOWN0, 4), (DOWN1, 3), (UP0, 2), (UP1, 1))
+    pair(1)
+    tick((ALIGN, 6), (DOWN0, 5), (DOWN1, 4), (UP0, 3), (UP1, 2), (OUT, 1))
+    pair(2)
+
+    def half_grads(mine):
+        left = n1s[core if mine else 1 - core].reshape(4 * 96, 4 * piece)
+        target = own[QKV] if mine else buffers[JOBS[QKV][5]]
+        for m in range(3):
+            value = dot(left, grad_at(m)[...]).astype(low)
+            for chip in range(4):
+                cy, cx = chip // 2, chip % 2
+                for h in range(2):
+                    i, k = (cx, cy) if h == 0 else (cy, cx)
+                    start = chip * 96 + h * 48
+                    target[h, i, k, :, pl.ds(m * half, half)] = value[start : start + 48]
+
+    half_grads(False)
+    stage(QKV, 0)
+    ready("low0", "low1", "low2", "unit1")
+
+    def pair_copy():
+        return remote_copy(e_at(partner), from_pair, pair_send, pair_recv, to_z1)
+
+    def end_copy(which, slot):
+        return remote_copy(e_at(slot), from_end.at[which], end_send.at[which], end_recv.at[which], to_z1)
+
+    def out_copy(which, slot):
+        return remote_copy(e_at(slot), total_in, out_send.at[which], out_recv, (dp, slot))
+
+    mid_near = 2 - clip
+    mid_far = 3 - 3 * clip
+    targets = (mid_far, mid_near)
+
+    def part_of(number, carry):
+        slot = jnp.where(
+            number == 0, mid_far, jnp.where(number == 1, mid_near, jnp.where(number == 2, partner, z))
+        )
+        where = pl.ds(pl.multiple_of(slot * piece, piece), piece)
+        value = dot(gq_ref[where, :], low_at(0)[...], NT)
+        value = value + dot(gk_ref[where, :], low_at(1)[...], NT)
+        value = value + dot(gv_ref[where, :], low_at(2)[...], NT)
+        e_at(slot)[...] = value.astype(low)
+
+        @pl.when(number == 3)
+        def _():
+            e_v[pl.ds(pl.multiple_of(clip * piece, piece), piece), :] = value
+
+        for which in range(2):
+
+            @pl.when(is_end & (number == which))
+            def _():
+                end_copy(which, targets[which]).start()
+
+        @pl.when(number == 2)
+        def _():
+            pair_copy().start()
+
+        return (carry[0] + total(value * unit1[where, :].astype(jnp.float32)), carry[1] + total(value))
+
+    for row, value in zip((N1_GAIN, N1_BIAS), lax.fori_loop(0, 4, part_of, (zero_row, zero_row))):
+        put_vector(row, 0, value)
+    for row, ref in ((Q_BIAS, gq_ref), (V_BIAS, gv_ref)):
+        value = total(ref[...])
+        value = jnp.concatenate([value, value], axis=1)
+        spot = lax.broadcasted_iota(jnp.int32, (1, width), 1)
+        put_vector(row, 0, jnp.where((spot < half) == (side == 0), value, 0.0))
+
+    vec_devices = (to_core, to_x, to_y, to_z1, to_z2)
+
+    def vec_copy(k):
+        return remote_copy(vec_out, vec_got.at[k], vsend.at[k], vrecv.at[k], vec_devices[k])
+
+    def vec_add(k):
+        vec_copy(k).wait()
+        vec_out[...] = vec_out[...] + vec_got[k]
+
+    vec_copy(0).start()
+    half_grads(True)
+    tick((DOWN0, 6), (DOWN1, 5), (UP0, 4), (UP1, 3), (OUT, 2), (QKV, 1))
+    vec_add(0)
+    vec_copy(1).start()
+
+    @pl.when(is_mid)
+    def _():
+        for which in range(2):
+            end_copy(which, targets[which]).wait_recv()
+            add_into(e_at(targets[which]), e_at(targets[which]), from_end.at[which])
+            out_copy(which, targets[which]).start()
+
+    tick((DOWN1, 6), (UP0, 5), (UP1, 4), (OUT, 3), (QKV, 2))
+    vec_add(1)
+    vec_copy(2).start()
+    tick((UP0, 6), (UP1, 5), (OUT, 4), (QKV, 3))
+    vec_add(2)
+    vec_copy(3).start()
+    tick((UP1, 6), (OUT, 5), (QKV, 4))
+    vec_add(3)
+    vec_copy(4).start()
+    tick((OUT, 6), (QKV, 5))
+    vec_add(4)
+
+    pair_copy().wait()
+    mine = pl.ds(pl.multiple_of(clip * piece, piece), piece)
+    theirs = pl.ds(pl.multiple_of((1 - clip) * piece, piece), piece)
+    e_v[mine, :] = e_v[mine, :] + from_pair[...].astype(jnp.float32)
+    out_copy(0, partner).wait_recv()
+    e_v[theirs, :] = total_in[...].astype(jnp.float32)
+
+    def last(at, carry):
+        one, inverse = norm_rows(tok[at, :].astype(jnp.float32))
+        value = mid_v[at, :] + norm_back(e_v[at, :], one, inverse, pack[N1_GAIN : N1_GAIN + 1, :])
+        grad_tokens[at, :] = value.astype(low)
+        return carry
+
+    chunks(last, 0)
+    tick((QKV, 6))
+
+    @pl.when(is_mid)
+    def _():
+        for which in range(2):
+            out_copy(which, targets[which]).wait_send()
+
+    @pl.when(is_end)
+    def _():
+        for which in range(2):
+            end_copy(which, targets[which]).wait_send()
+
+
+def back(small, large, out_rows):
+    tok = small[5]
+    rows, width = tok.shape
+    half, piece = width // 2, rows // 2
+    w_align, w_down, w_up, w_out, w_qkv = large[-5:]
+    wide, align = w_up.shape[1], w_align.shape[1]
+    low, wide_type = jnp.bfloat16, jnp.float32
+    vmem = pl.BlockSpec(memory_space=pltpu.VMEM)
+    hbm = pl.BlockSpec(memory_space=pl.ANY)
+    dma = pltpu.SemaphoreType.DMA
+    shapes = [(2, 2, 2, job[2] // 2, job[4]) for job in JOBS]
+    v = pltpu.VMEM
+    scratch = (
+        [v(shape, low) for shape in shapes]
+        + [v(shape, low) for shape in shapes]
+        + [v(shape[1:], low) for shape in shapes]
+        + [v(shape[2:], low) for shape in shapes]
+        + [v(shape[1:], low) for shape in shapes[:-1]]
+        + [v((3,) + shapes[-1][2:], low)]
+        + [v(shape, low) for shape in SEND_SHAPES]
+        + [v((5, PACK_ROWS, width), wide_type)]
+        + [
+            v(w_align.shape, low), v(w_down.shape, low), v(w_up.shape, low), v(w_out.shape, low),
+            v((rows, align), low), v((rows, width), low), v((rows, width), low), v((rows, width), low),
+            v((rows, wide), low),
+            v((2, 4, width // 8, rows), low), v((2, 4, wide // 8, rows), low),
+            v((2, 4, width // 8, rows), low), v((2, 4, width // 8, rows), low),
+            v((rows, width), wide_type), v((rows, width), wide_type), v((rows, width), low), v((rows, width), low),
+            v((2, 2, piece, half), low), v((4, piece, half), low), v((2, 4, width // 8, 4 * piece), low),
+            v((4 * piece, 128), wide_type), v((8, 4 * piece), wide_type), v((8, 4 * piece), wide_type),
+            v((4 * piece, 128), wide_type),
+            v((piece, width), low), v((2, piece, width), low), v((piece, width), low),
+        ]
+        + [dma((len(LOADS),))]
+        + [dma((COUNT, 2))] * 6
+        + [dma((COUNT, 2, 2))] * 2
+        + [dma((3, 2))] * 2
+        + [dma((COUNT + 5, 2))]
+        + [dma((5,))] * 2
+        + [dma((4,))] * 2
+        + [dma(())] * 2
+        + [dma((2,))] * 2
+        + [dma((2,)), dma(())]
+    )
+    struct = jax.ShapeDtypeStruct
+    return pl.pallas_call(
+        back_kernel,
+        name="back",
+        out_shape=[struct((rows, width), low), struct((PACK_ROWS, width), wide_type)]
+        + [struct(shape, low) for shape in out_rows],
+        in_specs=[vmem] * len(small) + [hbm] * len(large),
+        out_specs=[vmem, vmem] + [hbm] * 5,
+        scratch_shapes=scratch,
+        compiler_params=pltpu.CompilerParams(
+            collective_id=0, has_side_effects=True, vmem_limit_bytes=62 * 2**20
+        ),
+    )(*small, *large)
 
 
 def norm_forward(values, gain, shift):
@@ -261,6 +1374,77 @@
     )
 
 
+def local_kernels(
+    tokens, frame_counts, slot_mask, norm1_gain, norm1_bias, w_qkv, q_bias, v_bias, w_out, out_bias, norm2_gain,
+    norm2_bias, w_up, up_bias, w_down, down_bias, norm3_gain, norm3_bias, w_align, align_bias, cot_block, cot_align,
+):
+    clip_count, frame_dev, slot_count, width = tokens.shape
+    wide, align = w_up.shape[1], w_align.shape[1]
+    piece = frame_dev * slot_count
+    rows = clip_count * piece
+    pos = lax.axis_index("blk")
+    all_frames = jnp.arange(slot_mask.shape[1], dtype=jnp.int32)
+    valid = (all_frames[None, :, None] < frame_counts[:, None, None]) & (slot_mask > 0)
+    own_clip = lax.dynamic_index_in_dim(valid, pos // 2, 0, False)
+    key_bias = jnp.where(own_clip, 0.0, -1e30).astype(jnp.float32).reshape(1, -1)
+    own_mask = lax.dynamic_slice_in_dim(valid, pos * frame_dev, frame_dev, 1)
+    vis = own_mask.astype(jnp.float32).reshape(rows, 1)
+    vectors = [
+        norm1_gain, norm1_bias, q_bias, v_bias, out_bias, norm2_gain, norm2_bias, down_bias, norm3_gain, norm3_bias,
+        up_bias, align_bias,
+    ]
+    sizes = [vector.shape[0] for vector in vectors]
+    starts = [sum(sizes[:k]) for k in range(len(sizes))]
+    filler = jnp.zeros((PACK_ROWS * width - sum(sizes),), jnp.float32)
+    pack = jnp.concatenate(vectors + [filler]).reshape(PACK_ROWS, width)
+    tok = tokens.reshape(rows, width)
+    att, n1, unit1, qkv, own_att, lse = attend(tokens.reshape(clip_count, piece, width), pack, w_qkv, key_bias)
+    block_out, align_out, act_t, slope, unit2, inv2, unit3, inv3, normed2_t, normed3_t, att_t = feed(
+        tok, att, vis, pack, w_out, w_up, w_down, w_align
+    )
+
+    def by_share(array):
+        return array.reshape(4, 2, array.shape[0] // 8, rows)
+
+    grad_tokens, vec, *shares = back(
+        (vis, pack, key_bias.reshape(-1, 1), inv2, inv3, tok),
+        (
+            cot_align.reshape(rows, align), cot_block.reshape(rows, width), unit2, unit3, slope, by_share(normed3_t),
+            by_share(act_t), by_share(normed2_t), by_share(att_t), qkv, own_att.reshape(4 * piece, width // 2), lse,
+            n1.reshape(4 * piece, width), unit1.reshape(4 * piece, width), w_align, w_down, w_up, w_out, w_qkv,
+        ),
+        [(w.shape[0] // 8, w.shape[1]) for w in (w_qkv, w_out, w_up, w_down, w_align)],
+    )
+    flat = vec.reshape(-1)
+    (
+        grad_norm1_gain, grad_norm1_bias, grad_q_bias, grad_v_bias, grad_out_bias, grad_norm2_gain, grad_norm2_bias,
+        grad_down_bias, grad_norm3_gain, grad_norm3_bias, grad_up_bias, grad_align_bias,
+    ) = (flat[start : start + size] for start, size in zip(starts, sizes))
+    matrices = [share.astype(jnp.float32) for share in shares]
+    return (
+        block_out.reshape(tokens.shape),
+        align_out.reshape(cot_align.shape),
+        grad_tokens.reshape(tokens.shape),
+        grad_norm1_gain,
+        grad_norm1_bias,
+        matrices[0],
+        grad_q_bias,
+        grad_v_bias,
+        matrices[1],
+        grad_out_bias,
+        grad_norm2_gain,
+        grad_norm2_bias,
+        matrices[2],
+        grad_up_bias,
+        matrices[3],
+        grad_down_bias,
+        grad_norm3_gain,
+        grad_norm3_bias,
+        matrices[4],
+        grad_align_bias,
+    )
+
+
 def solution(mesh):
     in_specs = (
         P("dp", "blk", None, None),
@@ -308,4 +1492,6 @@
         P("dp", None),
         P(),
     )
-    return jax.shard_map(local, mesh=mesh, in_specs=in_specs, out_specs=out_specs, check_vma=False)
+    sizes = (mesh.shape["dp"], mesh.shape["blk"])
+    run = local_kernels if sizes == GRID else local
+    return jax.shard_map(run, mesh=mesh, in_specs=in_specs, out_specs=out_specs, check_vma=False)

time: 875 us -> 222 us (0.25)
  waiting for transfers between devices: 538 us -> 0 us
  Pallas kernels: 0 us -> 197 us
  matrix products: 117 us -> 0 us
  local copies, waits for them, and re-layouts: 105 us -> 15.3 us
  blocking collectives: 43.7 us -> 0 us
  other arithmetic: 49.1 us -> 8.21 us
  between operations: 15.3 us -> 0.73 us
    reduce_scatter x5 -> x0, waiting for transfers between devices: 300 us -> none  [the longest x1 78.2 us: local(): lax.psum_scatter(grad_w_up, 'dp', scatter_dimension=0, tiled=True)]
    pallas_call x0 -> x3, Pallas kernels: none -> 197 us  [the longest x1 128 us: back(): pl.pallas_call(back_kernel, name='back', out_shape=[struct((rows, width),...]
    unnamed x10 -> x0, waiting for transfers between devices: 133 us -> none
    dot_general x20 -> x0, matrix products: 105 us -> none  [the longest x5 32.1 us: weight_grad(): lax.dot_general(left, right, (((0,), (0,)), ((), ())), preferred_element_...]
    all_gather x2 -> x0, waiting for transfers between devices: 76.5 us -> none  [the longest x1 40.7 us: local(): lax.all_gather(values_local.reshape(block_shape), 'blk', axis=1, tiled=True)]
    reshape x12 -> x3, local copies, waits for them, and re-layouts: 53.3 us -> 1.43 us  [the longest x1 0.8 us: local_kernels(): vis = own_mask.astype(jnp.float32).reshape(rows, 1)]
    psum x1 -> x0, blocking collectives: 43.7 us -> none  [local(): lax.psum((grad_norm1_gain, grad_norm1_bias, grad_q_bias, grad_v_bias, gra...]
    convert_element_type x6 -> x0, local copies, waits for them, and re-layouts: 39.6 us -> none  [the longest x2 18.3 us: local(): key_terms.reshape(whole_shape).astype(jnp.bfloat16)]
  transfers between devices with their start and end apart: 9 -> 0, of which waited for: 9 -> 0; matrix products, arithmetic and copies ran while one was open for 12% -> 0% of each run, Pallas kernels for 0% -> 0%
where the time goes in v2:
time: 222 us; the launch traced here: 221 us
  Pallas kernels  197 us (89%)
  local copies, waits for them, and re-layouts  15.3 us (7%)
  other arithmetic  8.21 us (4%)
    pallas_call x1, Pallas kernels, back(): pl.pallas_call(back_kernel, name='back', out_shape=[struct((rows, width),...  128 us
    pallas_call x1, Pallas kernels, attend(): pl.pallas_call(attend_kernel, name='attend', out_shape=[jax.ShapeDtypeStr...  49.4 us
    pallas_call x1, Pallas kernels, feed(): pl.pallas_call(feed_kernel, name='feed', out_shape=[struct((rows, width),...  19.7 us
    unnamed x23, local copies, waits for them, and re-layouts  9.17 us
    convert_element_type x5, other arithmetic, local_kernels(): matrices = [share.astype(jnp.float32) for share in shares]  6.67 us

profile of v2, /device:TPU:0, one launch (start us, length us, event | category | flops | bytes accessed | tf_op | source)
XLA Modules:
  0.0 221.1 jit_solution(18295850901812166954)
XLA Ops:
  0.7 0.7 constant_dynamic-update-slice_fusion.12
  1.4 0.7 constant_dynamic-update-slice_fusion.11
  2.1 0.7 constant_dynamic-update-slice_fusion.10
  2.7 0.7 constant_dynamic-update-slice_fusion.9
  3.4 0.7 constant_dynamic-update-slice_fusion.8
  4.1 0.7 constant_dynamic-update-slice_fusion.7
  4.8 0.7 constant_dynamic-update-slice_fusion.6
  5.5 0.7 constant_dynamic-update-slice_fusion.5
  6.2 0.7 constant_dynamic-update-slice_fusion.4
  6.9 0.7 constant_dynamic-update-slice_fusion.3
  7.6 0.7 constant_dynamic-update-slice_fusion.2
  8.3 0.7 constant_dynamic-update-slice_fusion.1
  9.0 0.6 reshape.158.pack.refs_1_
  9.6 0.7 iota_compare_fusion
  10.4 0.8 compare_and_fusion
  11.2 0.7 select_n.39.key_bias
  11.8 49.4 %attend.1 = (bf16[2,2,192,384]{3,2,1,0:T(8,128)(2,1)}, bf16[4,192,768]{2,1,0:T(8,128)(2,1)}, bf16[4,192,768]{2,1,0:T(8,128)(2,1)}, bf16[3,768,384]{2,1,0:T(8,128...) custom-call(bf16[2,192,768]{2,1,0:T(8,128)(2,1)} %bitcast.14, f32[16,768]{1,0:T(8,128)} %reshape.158.pack.refs_1_, ...), custom_call_target="tpu_custom_call" | custom-call | tf_op jit(solution)/shard_map/attend/pallas_call | solution.py:366
  61.2 0.8 reshape.176.vis.refs_0_
  62.0 19.7 %feed.1 = (bf16[384,768]{1,0:T(8,128)(2,1)}, bf16[384,1024]{1,0:T(8,128)(2,1)}, bf16[3072,384]{1,0:T(8,128)(2,1)}, bf16[384,3072]{1,0:T(8,128)(2,1)}, bf16[384,7...) custom-call(bf16[384,768]{1,0:T(8,128)(2,1)} %bitcast.15, ...), custom_call_target="tpu_custom_call" | custom-call | tf_op jit(solution)/shard_map/feed/pallas_call | solution.py:162
  81.7 0.9 select_n.42.refs_2_
  82.6 127.8 %back.1 = (bf16[384,768]{1,0:T(8,128)(2,1)}, f32[16,768]{1,0:T(8,128)}, bf16[96,2304]{1,0:T(8,128)(2,1)}, bf16[96,768]{1,0:T(8,128)(2,1)}, bf16[96,3072]{1,0:T(8...) custom-call(f32[384,1]{1,0:T(8,128)} %reshape.176.vis.refs_0_, f32[16,768]{1,0:T(8,128)} %reshape.158.pack.refs_1_, ...), custom_call_target="tpu_custom_call" | custom-call | tf_op jit(solution)/shard_map/back/pallas_call | solution.py:1115
  210.5 0.0 copy-start.1
  210.5 1.9 slice_reduce_fusion
  212.4 0.0 copy-start.4
  212.4 0.0 copy-start
  212.4 2.0 convert_element_type.16
  214.5 1.6 convert_element_type.17
  216.1 0.0 copy-done.1
  216.1 0.0 copy-start.3
  216.1 0.0 copy-start.2
  216.1 1.1 convert_element_type.18
  217.2 0.0 copy-done.4
  217.2 0.6 slice.84
  217.8 0.0 copy-done
  217.8 1.1 convert_element_type.19
  218.9 0.0 copy-done.3
  218.9 0.8 convert_element_type.20
  219.7 0.6 slice.92
  220.3 0.0 copy-done.2
  220.3 0.8 copy.59
  (6 shorter events, 0.0 us)
Async XLA Ops:
  210.5 5.6 %copy-start.1 = (bf16[96,3072]{1,0:T(8,128)(2,1)S(1)}, bf16[96,3072]{1,0:T(8,128)(2,1)}, u32[]{:S(2)}) copy-start(bf16[96,3072]{1,0:T(8,128)(2,1)} %get-tuple-element.65) | copy-start | bytes 1769476
  212.4 4.8 %copy-start.4 = (f32[16,768]{1,0:T(8,128)S(1)}, f32[16,768]{1,0:T(8,128)}, u32[]{:S(2)}) copy-start(f32[16,768]{1,0:T(8,128)} %get-tuple-element.62) | copy-start | bytes 147460
  212.4 5.4 %copy-start = (bf16[384,768]{1,0:T(8,128)(2,1)S(1)}, bf16[384,768]{1,0:T(8,128)(2,1)}, u32[]{:S(2)}) copy-start(bf16[384,768]{1,0:T(8,128)(2,1)} %get-tuple-element.66) | copy-start | bytes 1769476
  216.1 2.8 %copy-start.3 = (bf16[96,1024]{1,0:T(8,128)(2,1)S(1)}, bf16[96,1024]{1,0:T(8,128)(2,1)}, u32[]{:S(2)}) copy-start(bf16[96,1024]{1,0:T(8,128)(2,1)} %get-tuple-element.67) | copy-start | bytes 589828
  216.1 4.2 %copy-start.2 = (bf16[384,768]{1,0:T(8,128)(2,1)S(1)}, bf16[384,768]{1,0:T(8,128)(2,1)}, u32[]{:S(2)}) copy-start(bf16[384,768]{1,0:T(8,128)(2,1)} %get-tuple-element.61) | copy-start | bytes 1769476
